TPU v7x, 128 devices: a whole 4x4x4 slice. The times are simulated.
128 devices in a mesh: tile: 32 (over x, z, core), grp: 4 (over y).
Axes of the slice: x: 4, y: 4, z: 4, core: 2. Of those that a mesh axis runs over, the one named last changes fastest.
Arguments:
- amplitudes: bfloat16 [2304, 128, 128], P('tile', 'grp'), may hold values from -6 to 6
- ladder_ints: bfloat16 [128, 128, 128, 128], P('grp', None, 'tile'), may hold values from -0.125 to 0.125
- cycle_ints: bfloat16 [48, 128, 48, 128], P(None, 'grp'), may hold values from -0.21875 to 0.21875
- occ_irrep: int32 [48], replicated, may hold values from 0 to 7
- virt_irrep: int32 [128], replicated, may hold values from 0 to 7, as said below
Outputs:
- residual: float32 [48, 48, 128, 128], P(None, 'grp', 'tile')
Inputs may be any that keep to these rules, and one draw needn't show every extreme that they name: `occ_irrep`: one of the eight irreducible representations of D2h for each occupied orbital. `virt_irrep`: one of the eight irreducible representations of D2h for each virtual orbital; each irrep labels at most 32 virtual orbitals, and one labels exactly 32.
All inputs are finite; a program needn't handle non-finite values.
Results may differ from a plain program's by a relative error of at most 0.0003.
Values may be sent and summed in bfloat16 or wider, within the bound.
A program may use at most 192 MiB of HBM per device.

v0:
```python
import jax
import jax.numpy as jnp
from jax import lax
from jax.sharding import PartitionSpec as P


def shards(amplitudes, ladder_ints, cycle_ints, occ_irrep, virt_irrep):
    rows = amplitudes.shape[0]
    part_c = amplitudes.shape[1]
    occ = occ_irrep.shape[0]
    virt = virt_irrep.shape[0]
    part_a = ladder_ints.shape[2]
    tile_at = lax.axis_index("tile")
    grp_at = lax.axis_index("grp")
    pair_ids = tile_at * rows + jnp.arange(rows, dtype=jnp.int32)
    pair_irrep = jnp.bitwise_xor(occ_irrep[pair_ids // occ], occ_irrep[pair_ids % occ])
    c_irrep = lax.dynamic_slice_in_dim(virt_irrep, grp_at * part_c, part_c)
    virt_pair = jnp.bitwise_xor(c_irrep[:, None], virt_irrep[None, :])
    allowed = pair_irrep[:, None, None] == virt_pair[None, :, :]
    masked = jnp.where(allowed, amplitudes, jnp.zeros((), jnp.bfloat16))
    ladder_flat = ladder_ints.reshape(part_c * virt, part_a * virt)
    gathered = lax.all_gather(masked, "tile", axis=0, tiled=True)
    ladder = jnp.dot(
        gathered.reshape(gathered.shape[0], part_c * virt),
        ladder_flat,
        preferred_element_type=jnp.float32,
    )
    cycle_slice = lax.dynamic_slice_in_dim(gathered, tile_at * part_a, part_a, 2)
    ladder = ladder.reshape(occ, occ, part_a, virt)
    cycle = jnp.einsum(
        "ikca,kcjb->ijab",
        cycle_slice.reshape(occ, occ, part_c, part_a),
        cycle_ints,
        preferred_element_type=jnp.float32,
    )
    partial_value = 0.5 * ladder + cycle
    a_irrep = lax.dynamic_slice_in_dim(virt_irrep, tile_at * part_a, part_a)
    part_j = occ // lax.axis_size("grp")
    j_irrep = lax.dynamic_slice_in_dim(occ_irrep, grp_at * part_j, part_j)
    combined = lax.psum_scatter(partial_value, "grp", scatter_dimension=1, tiled=True)
    swapped = jnp.swapaxes(
        lax.all_to_all(combined, "tile", split_axis=3, concat_axis=2, tiled=True), 2, 3
    )
    anti = combined - swapped
    anti = anti - jnp.swapaxes(
        lax.all_to_all(anti, "grp", split_axis=0, concat_axis=1, tiled=True), 0, 1
    )
    occ_pair = jnp.bitwise_xor(occ_irrep[:, None], j_irrep[None, :])
    out_pair = jnp.bitwise_xor(a_irrep[:, None], virt_irrep[None, :])
    out_allowed = occ_pair[:, :, None, None] == out_pair[None, None, :, :]
    return jnp.where(out_allowed, anti, jnp.zeros((), jnp.float32))


def solution(mesh):
    placed = (
        P("tile", "grp", None),
        P("grp", None, "tile", None),
        P(None, "grp", None, None),
        P(),
        P(),
    )
    return jax.shard_map(
        shards, mesh=mesh, in_specs=placed, out_specs=P(None, "grp", "tile", None), check_vma=False
    )
```

profile of v0, /device:TPU:1, one launch (start us, length us, event | category | flops | bytes accessed | tf_op | source)
XLA Modules:
  0.0 371.6 jit_solution(17743006877858818636)
XLA Ops:
  6.5 0.0 all-gather.2.cloned.1.call-start
  6.5 0.7 dynamic_slice.14
  7.3 0.7 broadcast_xor_fusion
  8.0 1.6 gather_fusion
  9.6 1.6 gather_fusion.1
  11.2 2.1 compare_select_fusion
  13.3 0.0 all-gather.2.cloned.1.call-update
  13.3 0.0 reduce-scatter.2.cloned.1.call-start
  13.4 4.9 %copy.75 = bf16[512,8,4,128]{3,1,2,0:T(8,128)(2,1)} copy(bf16[512,8,4,128]{3,2,1,0:T(4,128)(2,1)} %bitcast.58) | data formatting | bytes 8388608
  18.3 6.4 %copy.47 = bf16[512,4096]{1,0:T(8,128)(2,1)} copy(bf16[512,4096]{0,1:T(8,128)(2,1)} %bitcast.52) | data formatting | bytes 8388608 | tf_op jit(solution)/shard_map/dot_general | solution.py:23
  24.7 70.1 %all-gather.2.cloned.1.call-done = bf16[2304,32,128]{2,1,0:T(8,128)(2,1)} async-done(((bf16[72,32,128]{2,1,0:T(8,128)(2,1)}), bf16[2304,32,128]{2,1,0:T(8,128)(2,1)}) %all-gather.2.cloned.1.call-update) | async-done | bytes 18874384 | tf_op jit(solution)/shard_map/all_gather | solution.py:22
  94.8 18.6 %constant_dynamic-slice_fusion = bf16[2304,32,4]{2,1,0:T(8,128)(2,1)} fusion(bf16[2304,32,128]{2,1,0:T(8,128)(2,1)} %all-gather.2.cloned.1.call-done, s32[]{:T(128)S(6)} %select_n.65), kind=kLoop, calls=%fused_computation.26 | loop fusion | bytes 1179652 | tf_op jit(solution)/shard_map/dynamic_slice | solution.py:28
  113.4 23.0 %copy.61 = bf16[48,48,32,4,1]{1,0,2,4,3:T(8,128)(2,1)S(1)} copy(bf16[48,48,32,4,1]{3,2,1,0,4:T(8,128)(2,1)} %bitcast.51) | data formatting | bytes 1179648 | tf_op jit(solution)/shard_map/reshape | solution.py:32
  136.4 45.3 %fusion.8 = f32[48,4,48,128]{3,0,2,1:T(8,128)} fusion(bf16[48,48,32,4,1]{1,0,2,4,3:T(8,128)(2,1)S(1)} %copy.61, bf16[48,32,48,128]{3,2,1,0:T(8,128)(2,1)} %param.7), kind=kOutput, calls=%fused_computation.11 | convolution fusion | flops 3623878656 | bytes 24182784 | tf_op jit(solution)/shard_map/ikca,kcjb->ijab/dot_general | solution.py:30
  181.7 28.3 %reshape.175 = bf16[48,48,4096,1]{2,1,0,3:T(8,128)(2,1)} reshape(bf16[2304,32,128]{2,1,0:T(8,128)(2,1)} %all-gather.2.cloned.1.call-done) | data formatting | bytes 37748736 | tf_op jit(solution)/shard_map/dot_general | solution.py:23
  210.0 16.6 %bitcast_add_fusion = f32[48,48,4,128]{3,1,2,0:T(8,128)S(1)} fusion(f32[48,4,48,128]{3,0,2,1:T(8,128)} %fusion.8, bf16[4,128,4096,1]{2,1,0,3:T(8,128)(2,1)} %bitcast.59, bf16[48,48,4096,1]{2,1,0,3:T(8,128)(2,1)} %reshape.175), kind=kOutput, calls=%fused_computation.7 | convolution fusion | flops 9666035712 | bytes 32505856 | tf_op jit(solution)/shard_map/dot_general | solution.py:23
  226.6 4.9 %copy.51 = f32[48,48,4,128]{3,0,2,1:T(8,128)} copy(f32[48,48,4,128]{3,1,2,0:T(8,128)S(1)} %bitcast_add_fusion) | data formatting | bytes 9437184 | tf_op jit(solution)/shard_map/add | solution.py:36
  231.4 0.0 reduce-scatter.2.cloned.1.call-update
  231.5 50.3 %reduce-scatter.2.cloned.1.call-done = f32[48,12,4,128]{3,0,2,1:T(8,128)} async-done(((f32[48,48,4,128]{3,0,2,1:T(8,128)}), f32[48,12,4,128]{3,0,2,1:T(8,128)}) %reduce-scatter.2.cloned.1.call-update) | async-done | bytes 1179664 | tf_op jit(solution)/shard_map/reduce_scatter | solution.py:40
  281.8 3.2 copy.52
  285.0 4.4 %reshape.181 = f32[32,1,9216]{2,1,0:T(1,128)} reshape(f32[128,12,4,48]{3,2,1,0:T(4,128)S(1)} %bitcast.56) | data formatting | bytes 2359296
  289.4 7.9 %all-to-all-start = ((f32[32,1,9216]{2,1,0:T(1,128)}), f32[32,1,9216]{2,1,0:T(1,128)S(1)}, u32[]{:S(2)}, u32[]{:S(2)}) async-start(f32[32,1,9216]{2,1,0:T(1,128)} %reshape.181), calls=%async_computation.1 | async-start | bytes 2359296 | tf_op jit(solution)/shard_map/all_to_all | solution.py:42
  297.3 3.2 copy.55
  300.5 15.1 %all-to-all-done = f32[32,1,9216]{2,1,0:T(1,128)S(1)} async-done(((f32[32,1,9216]{2,1,0:T(1,128)}), f32[32,1,9216]{2,1,0:T(1,128)S(1)}, u32[]{:S(2)}, u32[]{:S(2)}) %all-to-all-start) | async-done | bytes 1179680 | tf_op jit(solution)/shard_map/all_to_all | solution.py:42
  315.6 0.5 broadcast.166
  316.1 4.7 %reduce = f32[32,9216]{1,0:T(8,128)} reduce(f32[32,1,9216]{2,1,0:T(1,128)S(1)} %all-to-all-done, f32[]{:T(128)} %broadcast.166), dimensions={1}, to_apply=%all_to_all.26.reduce_sub_computation | reduce | bytes 2359300 | tf_op jit(solution)/shard_map/all_to_all | solution.py:42
  320.8 4.3 %reshape.182 = f32[128,12,4,48]{3,2,1,0:T(4,128)S(1)} reshape(f32[32,9216]{1,0:T(8,128)} %reduce) | data formatting | bytes 2359296
  325.1 1.0 copy.53
  326.1 0.0 copy-start.1
  326.1 2.3 copy.54
  328.4 0.0 copy-done.1
  328.4 0.5 sub.13
  328.9 0.0 copy-start.2
  328.9 0.0 copy-start
  329.0 2.0 copy.56
  330.9 4.3 %all-to-all-start.1 = ((f32[48,12,4,128]{3,2,1,0:T(4,128)}), f32[48,12,4,128]{3,2,1,0:T(4,128)}, u32[]{:S(2)}, u32[]{:S(2)}) async-start(f32[48,12,4,128]{3,2,1,0:T(4,128)} %copy.56), calls=%async_computation.2 | async-start | bytes 2359296 | tf_op jit(solution)/shard_map/all_to_all | solution.py:46
  335.2 0.0 copy-done.2
  335.2 0.1 dynamic_slice.13
  335.3 0.0 copy-done
  335.3 0.1 dynamic_slice.12
  335.4 0.1 broadcast_xor_fusion.2
  335.4 0.1 broadcast_xor_fusion.1
  335.5 16.1 %all-to-all-done.1 = f32[48,12,4,128]{3,2,1,0:T(4,128)} async-done(((f32[48,12,4,128]{3,2,1,0:T(4,128)}), f32[48,12,4,128]{3,2,1,0:T(4,128)}, u32[]{:S(2)}, u32[]{:S(2)}) %all-to-all-start.1) | async-done | bytes 1179680 | tf_op jit(solution)/shard_map/all_to_all | solution.py:46
  351.6 2.4 copy.57
  354.0 3.2 copy.58
  357.2 4.3 %fusion.5 = f32[48,12,4,128]{0,3,2,1:T(8,128)} fusion(f32[48,12,4,128]{0,3,2,1:T(8,128)S(1)} %sub.13, f32[12,48,4,128]{1,3,2,0:T(8,128)} %copy.58, s32[4,128]{1,0:T(4,128)S(1)} %broadcast_xor_fusion.2, s32[48,12]{0,1:T(8,128)S(1)} %broadcast_xor_fusion.1), kind=kLoop, calls=%fused_computation.10 | loop fusion | flops 884736 | bytes 3543296 | tf_op jit(solution)/shard_map/jit(_where)/select_n | solution.py:51
  361.5 3.1 copy.59
  (4 shorter events, 0.0 us)
Async XLA Ops:
  6.5 88.3 %all-gather.2.cloned.1.call-start = ((), (), s32[]{:S(2)}) async-start(), calls=%async_computation.3 | async-start | bytes 19464192 | tf_op jit(solution)/shard_map/all_gather | solution.py:22
  13.3 268.4 %reduce-scatter.2.cloned.1.call-start = ((), (), s32[]{:S(2)}) async-start(), calls=%async_computation.4 | async-start | bytes 5898240 | tf_op jit(solution)/shard_map/reduce_scatter | solution.py:40
  289.4 26.2 %all-to-all-start = ((f32[32,1,9216]{2,1,0:T(1,128)}), f32[32,1,9216]{2,1,0:T(1,128)S(1)}, u32[]{:S(2)}, u32[]{:S(2)}) async-start(f32[32,1,9216]{2,1,0:T(1,128)} %reshape.181), calls=%async_computation.1 | async-start | bytes 2359296 | tf_op jit(solution)/shard_map/all_to_all | solution.py:42
  326.1 2.3 copy-start.1
  328.9 6.3 %copy-start.2 = (s32[128]{0:T(128)S(1)}, s32[128]{0:T(128)}, u32[]{:S(2)}) copy-start(s32[128]{0:T(128)} %param.9) | copy-start | bytes 1540
  328.9 6.3 %copy-start = (s32[48]{0:T(128)S(1)}, s32[48]{0:T(128)}, u32[]{:S(2)}) copy-start(s32[48]{0:T(128)} %param.8) | copy-start | bytes 580
  330.9 20.7 %all-to-all-start.1 = ((f32[48,12,4,128]{3,2,1,0:T(4,128)}), f32[48,12,4,128]{3,2,1,0:T(4,128)}, u32[]{:S(2)}, u32[]{:S(2)}) async-start(f32[48,12,4,128]{3,2,1,0:T(4,128)} %copy.56), calls=%async_computation.2 | async-start | bytes 2359296 | tf_op jit(solution)/shard_map/all_to_all | solution.py:46
Sparse Core Ops, SparseCore 0:
  13.5 81.3 all-gather.1
  231.6 50.1 reduce-scatter.1
where the time goes:
time: 377 us; the launch traced here: 372 us
  waiting for transfers between devices  152 us (40%)
  local copies, waits for them, and re-layouts  120 us (32%)
  matrix products  61.8 us (16%)
  between operations  13.7 us (4%)
  other arithmetic  12.5 us (3%)
  starting transfers between devices  12.2 us (3%)
    all_gather x1, waiting for transfers between devices, shards(): gathered = lax.all_gather(masked, 'tile', axis=0, tiled=True)  70.1 us
    reduce_scatter x1, waiting for transfers between devices, shards(): lax.psum_scatter(partial_value, 'grp', scatter_dimension=1, tiled=True)  50.3 us
    dot_general x1, matrix products, shards(): jnp.einsum('ikca,kcjb->ijab', cycle_slice.reshape(occ, occ, part_c, part_...  45.3 us
    dot_general x2, local copies, waits for them, and re-layouts, shards(): jnp.dot(gathered.reshape(gathered.shape[0], part_c * virt), ladder_flat,...  34.7 us
    reshape x1, local copies, waits for them, and re-layouts, shards(): cycle_slice.reshape(occ, occ, part_c, part_a)  23 us
    dynamic_slice x1, local copies, waits for them, and re-layouts, shards(): lax.dynamic_slice_in_dim(gathered, tile_at * part_a, part_a, 2)  18.6 us
    dot_general x1, matrix products, shards(): jnp.dot(gathered.reshape(gathered.shape[0], part_c * virt), ladder_flat,...  16.6 us
    all_to_all x1, waiting for transfers between devices, shards(): lax.all_to_all(anti, 'grp', split_axis=0, concat_axis=1, tiled=True)  16.1 us
  transfers between devices with their start and end apart: 4, of which 4 were waited for; matrix products, arithmetic and copies ran while one was open for 4% of the time, Pallas kernels for 0%

commit v1 on v0

v1 whole, which is shorter than its diff:
```python
import jax
import jax.numpy as jnp
from jax import lax
from jax.experimental import pallas as pl
from jax.experimental.pallas import tpu as pltpu
from jax.sharding import PartitionSpec as P

NO = 48
NV = 128
SLOTS = 32
PART_C = 32
PART_A = 4
PART_J = 12
TILES = 32
GRPS = 4
ROWS = 72
IRREPS = 8
F32 = jnp.float32
BF16 = jnp.bfloat16
I32 = jnp.int32


def iota(shape, axis):
    return lax.broadcasted_iota(I32, shape, axis)


def lanes_at(values, index):
    return jnp.take_along_axis(values, index, axis=1, mode="promise_in_bounds")


def spread(selector, values):
    return jnp.dot(selector.astype(BF16), values.astype(BF16), preferred_element_type=F32).astype(I32)


def pick_rows(table, which):
    picked = jnp.broadcast_to(table[0:1], which.shape)
    for irrep in range(1, IRREPS):
        picked = jnp.where(which == irrep, jnp.broadcast_to(table[irrep : irrep + 1], which.shape), picked)
    return picked


def column_of(virt_row):
    return jnp.broadcast_to(virt_row, (NV, NV)).astype(F32).T.astype(I32)


def pack_body(occ_s, virt_ref, t_ref, out_ref, table_ref, index_ref, column_ref, rows_ref):
    row = jnp.broadcast_to(virt_ref[...], (NV, NV))
    col = column_of(virt_ref[...])
    column_ref[...] = col
    sub = iota((NV, NV), 0)
    lane = iota((NV, NV), 1)
    same = row == col
    rank_col = jnp.sum(jnp.where(same & (lane < sub), 1.0, 0.0), axis=1, keepdims=True)
    rank_row = jnp.sum(jnp.where(same & (sub < lane), 1.0, 0.0), axis=0, keepdims=True)
    hit = jnp.broadcast_to(rank_col, (NV, NV)).astype(I32) == lane % SLOTS
    subf = sub.astype(F32)
    entries = [
        jnp.sum(jnp.where(hit & (col == irrep), subf, 0.0), axis=0, keepdims=True)
        for irrep in range(IRREPS)
    ]
    table = jnp.concatenate(entries, axis=0).astype(I32)
    table_ref[0:8] = table
    table_ref[8:16] = jnp.broadcast_to(rank_row, (8, NV)).astype(I32)
    c_col = column_ref[pl.ds(pl.multiple_of(lax.axis_index("grp") * PART_C, PART_C), PART_C)]
    for irrep in range(IRREPS):
        index_ref[irrep] = pick_rows(table, c_col ^ irrep)
    first = lax.axis_index("tile") * ROWS
    quarter = iota((8, NV), 1) // SLOTS

    def one_row(r, carry):
        pair = first + r
        irrep = occ_s[pair // NO] ^ occ_s[pair % NO]
        got = lanes_at(t_ref[r].astype(F32), index_ref[irrep])
        row = got[24:32]
        for q in (2, 1, 0):
            row = jnp.where(quarter == q, got[8 * q : 8 * q + 8], row)
        rows_ref[pl.ds(pl.multiple_of(r * 8, 8), 8)] = row
        return carry

    lax.fori_loop(0, ROWS, one_row, 0, unroll=8)
    for block in range(ROWS // 8):
        for half in range(4):
            pair_of = [
                rows_ref[pl.ds(block * 64 + 2 * half + odd, 8, stride=8)] for odd in range(2)
            ]
            out_ref[block, half] = jnp.concatenate(pair_of, axis=0).astype(BF16)


def pack(occ, virt_row, amplitudes):
    return pl.pallas_call(
        pack_body,
        out_shape=(
            jax.ShapeDtypeStruct((ROWS // 8, 4, 16, NV), BF16),
            jax.ShapeDtypeStruct((16, NV), I32),
        ),
        in_specs=[
            pl.BlockSpec(memory_space=pltpu.SMEM),
            pl.BlockSpec(memory_space=pltpu.VMEM),
            pl.BlockSpec(memory_space=pltpu.VMEM),
        ],
        out_specs=(pl.BlockSpec(memory_space=pltpu.VMEM), pl.BlockSpec(memory_space=pltpu.VMEM)),
        scratch_shapes=[
            pltpu.VMEM((IRREPS, PART_C, NV), I32),
            pltpu.VMEM((NV, NV), I32),
            pltpu.VMEM((ROWS * 8, NV), F32),
        ],
        compiler_params=pltpu.CompilerParams(vmem_limit_bytes=32 * 2**20),
        name="pack",
    )(occ, virt_row, amplitudes)


C_STEP = 4


def ladder_prep_body(virt_s, virt_ref, table_ref, v_ref, out_ref, index_ref, perm_ref):
    step = pl.program_id(0)
    wide = NV * PART_A
    first_a = lax.axis_index("tile") * PART_A

    @pl.when(step == 0)
    def _():
        col = column_of(virt_ref[...])
        sub = iota((wide, NV), 0)
        lane = iota((wide, NV), 1)
        of_d = spread(lane == sub // PART_A, col)
        of_a = spread(lane == first_a + sub % PART_A, col)
        both = of_d ^ of_a
        table = table_ref[0:8]
        for irrep in range(IRREPS):
            index_ref[irrep] = pick_rows(table, both ^ irrep)
        repeat = iota((NV, wide), 1) // PART_A == iota((NV, wide), 0)
        irrep_row = spread(jnp.broadcast_to(virt_ref[...], (8, NV)), repeat)[0:1]
        rank_row = spread(table_ref[8:16], repeat)[0:1]
        at = iota((IRREPS * SLOTS, wide), 0)
        perm_ref[...] = jnp.where((irrep_row == at // SLOTS) & (rank_row == at % SLOTS), 1.0, 0.0).astype(BF16)

    own = iota((wide, NV), 1) // SLOTS == iota((wide, NV), 0) % PART_A
    for u in range(C_STEP):
        c = step * C_STEP + u
        irrep_c = virt_s[lax.axis_index("grp") * PART_C + c]
        got = lanes_at(v_ref[u].astype(F32), index_ref[irrep_c])
        compact = jnp.where(own, got, 0.0).astype(BF16)
        ordered = jnp.dot(perm_ref[...], compact, preferred_element_type=F32).astype(BF16)
        start = pl.multiple_of((c % 8) * NV + (c // 8) * SLOTS, SLOTS)
        for irrep in range(IRREPS):
            out_ref[irrep_c ^ irrep, pl.ds(start, SLOTS)] = ordered[irrep * SLOTS : (irrep + 1) * SLOTS]


def ladder_prep(virt, virt_row, table, ladder_rows):
    wide = NV * PART_A
    return pl.pallas_call(
        ladder_prep_body,
        grid=(PART_C // C_STEP,),
        out_shape=jax.ShapeDtypeStruct((IRREPS, PART_C * SLOTS, NV), BF16),
        in_specs=[
            pl.BlockSpec(memory_space=pltpu.SMEM),
            pl.BlockSpec((1, NV), lambda s: (0, 0)),
            pl.BlockSpec((16, NV), lambda s: (0, 0)),
            pl.BlockSpec((C_STEP, wide, NV), lambda s: (s, 0, 0)),
        ],
        out_specs=pl.BlockSpec((IRREPS, PART_C * SLOTS, NV), lambda s: (0, 0, 0)),
        scratch_shapes=[
            pltpu.VMEM((IRREPS, wide, NV), I32),
            pltpu.VMEM((IRREPS * SLOTS, wide), BF16),
        ],
        compiler_params=pltpu.CompilerParams(vmem_limit_bytes=40 * 2**20),
        cost_estimate=pl.CostEstimate(flops=2 * 10**9, bytes_accessed=7 * 10**6, transcendentals=0),
        name="ladder_prep",
    )(virt, virt_row, table, ladder_rows)


KC = NO * PART_C
KC_STEP = 64


def cycle_prep_body(w_ref, out_ref, rows_ref):
    for u in range(KC_STEP // 16):
        rows_ref[u] = w_ref[16 * u : 16 * u + 16].astype(F32).reshape(16 * NO, NV)
        for j in range(NO):
            out_ref[j, 16 * u : 16 * u + 16] = rows_ref[u, pl.ds(j, 16, stride=NO)].astype(BF16)


def cycle_prep(cycle_rows):
    return pl.pallas_call(
        cycle_prep_body,
        grid=(KC // KC_STEP,),
        out_shape=jax.ShapeDtypeStruct((NO, KC, NV), BF16),
        in_specs=[pl.BlockSpec((KC_STEP, NO, NV), lambda s: (s, 0, 0))],
        out_specs=pl.BlockSpec((NO, KC_STEP, NV), lambda s: (0, s, 0)),
        scratch_shapes=[pltpu.VMEM((KC_STEP // 16, 16 * NO, NV), F32)],
        compiler_params=pltpu.CompilerParams(vmem_limit_bytes=40 * 2**20),
        cost_estimate=pl.CostEstimate(flops=2 * 10**9, bytes_accessed=38 * 10**6, transcendentals=0),
        name="cycle_prep",
    )(cycle_rows)


J_STEP = 4
I_STEP = 6


def contract_body(occ_s, virt_ref, table_ref, t_ref, v_ref, w_ref, out_ref, ladder_ref, cut_ref, left_ref, index_ref, total_ref):
    step = pl.program_id(0)
    first_a = lax.axis_index("tile") * PART_A
    first_c = lax.axis_index("grp") * PART_C
    lane48 = iota((NO, NV), 1)

    @pl.when(step == 0)
    def _():
        sub48 = iota((NO, NV), 0)
        occ_col = jnp.zeros((NO, NV), I32)
        for i in range(NO):
            occ_col = jnp.where(sub48 == i, occ_s[i], occ_col)
        table = table_ref[0:8]
        virt8 = jnp.broadcast_to(virt_ref[...], (8, NV))
        sub = iota((NV, NV), 0)
        lane = iota((NV, NV), 1)
        of_a = sub == first_a + lane // PART_C
        of_c = sub == first_c + lane % PART_C
        a_irrep = spread(virt8, of_a)
        ac_irrep = (a_irrep ^ spread(virt8, of_c))[0:1]
        a_rank = spread(table_ref[8:16], of_a)[0:1]
        deep = (PART_C * SLOTS, NV)
        at = iota(deep, 0)
        c_at = 8 * ((at % NV) // SLOTS) + at // NV
        cut = jnp.where((c_at == iota(deep, 1) % PART_C) & (a_rank == at % SLOTS), 1.0, 0.0).astype(BF16)
        lane_g = lane48
        for a in range(PART_A):
            irrep_a = a_irrep[0:1, a * PART_C : a * PART_C + 1]
            base = occ_col ^ irrep_a
            for irrep in range(IRREPS):
                index_ref[irrep, a * NO : (a + 1) * NO] = pick_rows(table, base ^ irrep)

        def block(n, carry):
            got = t_ref[pl.ds(n * (I_STEP * 6), I_STEP * 6)].astype(F32)
            m_rows = I_STEP * NO
            planes = [
                got[:, m // 2, (m % 2) * 8 : (m % 2) * 8 + 8].reshape(m_rows, NV).astype(BF16)
                for m in range(8)
            ]
            left = jnp.concatenate(planes, axis=1)
            pair_irrep = jnp.concatenate([occ_col ^ occ_s[n * I_STEP + u] for u in range(I_STEP)], axis=0)
            total = jnp.zeros((m_rows, NV), F32)
            for pair in range(4):
                right = jnp.concatenate([v_ref[2 * pair], v_ref[2 * pair + 1]], axis=1)
                both = jnp.dot(left, right, preferred_element_type=F32)
                total = jnp.where(pair_irrep == 2 * pair, both[:, :NV], total)
                total = jnp.where(pair_irrep == 2 * pair + 1, both[:, NV:], total)
            rows = pl.ds(pl.multiple_of(n * m_rows, m_rows), m_rows)
            ladder_ref[rows] = total
            piece = jnp.dot(left, cut, preferred_element_type=F32)
            cut_ref[rows] = jnp.where(pair_irrep == ac_irrep, piece, 0.0)
            return carry

        lax.fori_loop(0, NO // I_STEP, block, 0)
        for chunk in range(NO // 4):
            parts = [cut_ref[pl.ds(4 * chunk + u, NO, stride=NO)] for u in range(4)]
            turned = [
                [parts[u] if d == 0 else pltpu.roll(parts[u], PART_C * d, 1) for d in range(4)]
                for u in range(4)
            ]
            for a in range(PART_A):
                piece = turned[3][(3 - a) % 4]
                for u in (2, 1, 0):
                    piece = jnp.where(lane48 // PART_C == u, turned[u][(u - a) % 4], piece)
                left_ref[a * NO : (a + 1) * NO, chunk * NV : (chunk + 1) * NV] = piece.astype(BF16)

    for u in range(J_STEP // 2):
        right = jnp.concatenate([w_ref[2 * u], w_ref[2 * u + 1]], axis=1)
        both = jnp.dot(left_ref[...], right, preferred_element_type=F32)
        for odd in range(2):
            j = step * J_STEP + 2 * u + odd
            got = lanes_at(both[:, odd * NV : (odd + 1) * NV], index_ref[occ_s[j]])
            value = got[3 * NO :]
            for a in (2, 1, 0):
                value = jnp.where(lane48 // SLOTS == a, got[a * NO : (a + 1) * NO], value)
            value = value + 0.5 * ladder_ref[pl.ds(j, NO, stride=NO)]
            total_ref[pl.ds(pl.multiple_of(j * NO, NO), NO)] = value

    @pl.when(step == pl.num_programs(0) - 1)
    def _():
        def anti(j, carry):
            rows = pl.ds(pl.multiple_of(j * NO, NO), NO)
            out_ref[j] = total_ref[rows] - total_ref[pl.ds(j, NO, stride=NO)]
            return carry

        lax.fori_loop(0, NO, anti, 0, unroll=4)


def contract(occ, virt_row, table, gathered, ladder_compact, cycle_compact):
    pairs = NO * NO
    return pl.pallas_call(
        contract_body,
        grid=(NO // J_STEP,),
        out_shape=jax.ShapeDtypeStruct((NO, NO, NV), F32),
        in_specs=[
            pl.BlockSpec(memory_space=pltpu.SMEM),
            pl.BlockSpec((1, NV), lambda s: (0, 0)),
            pl.BlockSpec((16, NV), lambda s: (0, 0)),
            pl.BlockSpec(gathered.shape, lambda s: (0, 0, 0, 0), pipeline_mode=pl.Buffered(1)),
            pl.BlockSpec(ladder_compact.shape, lambda s: (0, 0, 0), pipeline_mode=pl.Buffered(1)),
            pl.BlockSpec((J_STEP, KC, NV), lambda s: (s, 0, 0)),
        ],
        out_specs=pl.BlockSpec((NO, NO, NV), lambda s: (0, 0, 0)),
        scratch_shapes=[
            pltpu.VMEM((pairs, NV), F32),
            pltpu.VMEM((pairs, NV), F32),
            pltpu.VMEM((PART_A * NO, KC), BF16),
            pltpu.VMEM((IRREPS, PART_A * NO, NV), I32),
            pltpu.VMEM((pairs, NV), F32),
        ],
        compiler_params=pltpu.CompilerParams(vmem_limit_bytes=48 * 2**20),
        name="contract",
    )(occ, virt_row, table, gathered, ladder_compact, cycle_compact)


def expand_body(occ_s, virt_ref, table_ref, z_ref, out_ref):
    first_a = lax.axis_index("tile") * PART_A
    first_j = lax.axis_index("grp") * PART_J
    sub48 = iota((NO, NV), 0)
    occ_col = jnp.zeros((NO, NV), I32)
    for i in range(NO):
        occ_col = jnp.where(sub48 == i, occ_s[i], occ_col)
    virt_row = jnp.broadcast_to(virt_ref[...], (NO, NV))
    rank_row = jnp.broadcast_to(table_ref[8:9], (NO, NV))
    virt8 = jnp.broadcast_to(virt_ref[...], (8, NV))
    a_irrep = spread(virt8, iota((NV, NV), 0) == first_a + iota((NV, NV), 1) // PART_C)

    def one(j, carry):
        irrep_j = occ_s[first_j + j]
        for a in range(PART_A):
            got = lanes_at(z_ref[j], rank_row + a * SLOTS)
            want = virt_row ^ a_irrep[0:1, a * PART_C : a * PART_C + 1] ^ irrep_j
            out_ref[a, j] = jnp.where(occ_col == want, got, 0.0)
        return carry

    lax.fori_loop(0, PART_J, one, 0)


def expand(occ, virt_row, table, reduced):
    return pl.pallas_call(
        expand_body,
        out_shape=jax.ShapeDtypeStruct((PART_A, PART_J, NO, NV), F32),
        in_specs=[pl.BlockSpec(memory_space=pltpu.SMEM)] + [pl.BlockSpec(memory_space=pltpu.VMEM)] * 3,
        out_specs=pl.BlockSpec(memory_space=pltpu.VMEM),
        compiler_params=pltpu.CompilerParams(vmem_limit_bytes=32 * 2**20),
        name="expand",
    )(occ, virt_row, table, reduced)


def shards(amplitudes, ladder_ints, cycle_ints, occ_irrep, virt_irrep):
    virt_row = virt_irrep.reshape(1, NV)
    packed, table = pack(occ_irrep, virt_row, amplitudes)
    gathered = lax.all_gather(packed, "tile", axis=0, tiled=True)
    ladder_compact = ladder_prep(virt_irrep, virt_row, table, ladder_ints.reshape(PART_C, NV * PART_A, NV))
    cycle_compact = cycle_prep(cycle_ints.reshape(KC, NO, NV))
    partial_sum = contract(occ_irrep, virt_row, table, gathered, ladder_compact, cycle_compact)
    reduced = lax.psum_scatter(partial_sum, "grp", scatter_dimension=0, tiled=True)
    dense = expand(occ_irrep, virt_row, table, reduced)
    swapped = lax.all_to_all(dense, "tile", split_axis=3, concat_axis=0, tiled=True)
    return jnp.transpose(dense, (2, 1, 0, 3)) - jnp.transpose(swapped, (2, 1, 3, 0))


def solution(mesh):
    placed = (
        P("tile", "grp", None),
        P("grp", None, "tile", None),
        P(None, "grp", None, None),
        P(),
        P(),
    )
    return jax.shard_map(
        shards, mesh=mesh, in_specs=placed, out_specs=P(None, "grp", "tile", None), check_vma=False
    )
```

time: 377 us -> 177 us (0.47); the launches traced: 372 us -> 176 us
  waiting for transfers between devices: 152 us -> 36.4 us
  local copies, waits for them, and re-layouts: 120 us -> 27.1 us
  Pallas kernels: 0 us -> 67.7 us
  matrix products: 61.8 us -> 0 us
  blocking collectives: 0 us -> 27.7 us
  starting transfers between devices: 12.2 us -> 0.04 us
  other arithmetic: 12.5 us -> 3.7 us
    pallas_call x0 -> x5, Pallas kernels: none -> 67.7 us  [the longest x1 26.5 us: contract(): pl.pallas_call(contract_body, grid=(NO // J_STEP,), out_shape=jax.ShapeDt...]
    dot_general x2 -> x0, matrix products: 61.8 us -> none  [the longest x1 45.3 us: shards(): jnp.einsum('ikca,kcjb->ijab', cycle_slice.reshape(occ, occ, part_c, part_...]
    all_gather x1, waiting for transfers between devices: 70.1 us -> 14.5 us  [shards(): gathered = lax.all_gather(packed, 'tile', axis=0, tiled=True)]
    dot_general x2 -> x0, local copies, waits for them, and re-layouts: 34.7 us -> none  [shards(): jnp.dot(gathered.reshape(gathered.shape[0], part_c * virt), ladder_flat,...]
    all_to_all x2 -> x0, waiting for transfers between devices: 31.2 us -> none  [the longest x1 16.1 us: shards(): lax.all_to_all(anti, 'grp', split_axis=0, concat_axis=1, tiled=True)]
    reduce_scatter x1, waiting for transfers between devices: 50.3 us -> 21.9 us  [shards(): lax.psum_scatter(partial_sum, 'grp', scatter_dimension=0, tiled=True)]
    all_to_all x0 -> x1, blocking collectives: none -> 27.7 us  [shards(): lax.all_to_all(dense, 'tile', split_axis=3, concat_axis=0, tiled=True)]
    reshape x1 -> x0, local copies, waits for them, and re-layouts: 23 us -> none  [shards(): cycle_slice.reshape(occ, occ, part_c, part_a)]
  transfers between devices with their start and end apart: 4 -> 2, of which waited for: 4 -> 2; matrix products, arithmetic and copies ran while one was open for 4% -> 0% of each run, Pallas kernels for 0% -> 21%
where the time goes in v1:
time: 177 us; the launch traced here: 176 us
  Pallas kernels  67.7 us (38%)
  waiting for transfers between devices  36.4 us (21%)
  blocking collectives  27.7 us (16%)
  local copies, waits for them, and re-layouts  27.1 us (15%)
  between operations  13.5 us (8%)
  other arithmetic  3.7 us (2%)
    all_to_all x1, blocking collectives, shards(): lax.all_to_all(dense, 'tile', split_axis=3, concat_axis=0, tiled=True)  27.7 us
    pallas_call x1, Pallas kernels, contract(): pl.pallas_call(contract_body, grid=(NO // J_STEP,), out_shape=jax.ShapeDt...  26.5 us
    pallas_call x1, Pallas kernels, cycle_prep(): pl.pallas_call(cycle_prep_body, grid=(KC // KC_STEP,), out_shape=jax.Shap...  25.6 us
    reduce_scatter x1, waiting for transfers between devices, shards(): lax.psum_scatter(partial_sum, 'grp', scatter_dimension=0, tiled=True)  21.9 us
    all_gather x1, waiting for transfers between devices, shards(): gathered = lax.all_gather(packed, 'tile', axis=0, tiled=True)  14.5 us
    unnamed x16, local copies, waits for them, and re-layouts  12.6 us
    pallas_call x1, Pallas kernels, ladder_prep(): pl.pallas_call(ladder_prep_body, grid=(PART_C // C_STEP,), out_shape=jax....  10.5 us
    all_to_all x4, local copies, waits for them, and re-layouts, shards(): lax.all_to_all(dense, 'tile', split_axis=3, concat_axis=0, tiled=True)  9.7 us
  transfers between devices with their start and end apart: 2, of which 2 were waited for; matrix products, arithmetic and copies ran while one was open for 0% of the time, Pallas kernels for 21%

profile of v1, /device:TPU:1, one launch (start us, length us, event | category | flops | bytes accessed | tf_op | source)
XLA Modules:
  0.0 176.1 jit_solution(16147095959339272671)
XLA Ops:
  6.5 0.0 all-gather.2.cloned.1.call-start
  6.5 0.0 copy-start
  6.5 1.1 copy-done
  7.6 0.0 copy-start.2
  7.6 0.7 copy-done.2
  8.3 0.0 copy-start.4
  8.3 0.7 copy-done.4
  8.9 3.0 %pack.1 = (bf16[9,4,16,128]{3,2,1,0:T(8,128)(2,1)}, s32[16,128]{1,0:T(8,128)S(1)}) custom-call(s32[48]{0:T(128)S(1)} %copy-done.2, s32[1,128]{1,0:T(1,128)S(1)} %bitcast.13, bf16[72,32,128]{2,1,0:T(8,128)(2,1)S(1)} %copy-done), custom_call_target="tpu_custom_call" | custom-call | tf_op jit(solution)/shard_map/pack/pallas_call | solution.py:90
  11.9 0.0 all-gather.2.cloned.1.call-update
  11.9 0.0 reduce-scatter.2.cloned.1.call-start
  12.0 0.0 copy-start.5
  12.0 0.0 copy-start.6
  12.0 25.6 %cycle_prep.1.w_ref = bf16[48,1536,128]{2,1,0:T(8,128)(2,1)} custom-call(bf16[1536,48,128]{2,1,0:T(8,128)(2,1)} %bitcast.18), custom_call_target="tpu_custom_call" | custom-call | flops 2000000000 | bytes 38000000 | tf_op jit(solution)/shard_map/cycle_prep/pallas_call | solution.py:184
  37.6 0.0 copy-done.5
  37.6 0.0 copy-done.6
  37.6 0.0 copy-start.3
  37.6 10.5 %ladder_prep.1.v_ref = bf16[8,1024,128]{2,1,0:T(8,128)(2,1)S(1)} custom-call(s32[128]{0:T(128)S(1)} %copy-done.5, s32[1,128]{1,0:T(1,128)S(1)} %bitcast.14, s32[16,128]{1,0:T(8,128)S(1)} %get-tuple-element.7.table_ref, bf16[32,512,128]{2,1,0:T(8,128)(2,1)S(1)} %bitcast.17), custom_call_target="tpu_custom_call" | custom-call | flops 2000000000 | bytes 7000000 | tf_op jit(solution)/shard_map/ladder_prep/pallas_call | solution.py:151
  48.1 14.5 %all-gather.2.cloned.1.call-done.t_ref = bf16[288,4,16,128]{3,2,1,0:T(8,128)(2,1)} async-done(((bf16[9,4,16,128]{3,2,1,0:T(8,128)(2,1)}), bf16[288,4,16,128]{3,2,1,0:T(8,128)(2,1)}) %all-gather.2.cloned.1.call-update) | async-done | bytes 4718608 | tf_op jit(solution)/shard_map/all_gather | solution.py:353
  62.7 0.0 copy-done.3
  62.7 26.5 %contract.1 = f32[48,48,128]{2,1,0:T(8,128)} custom-call(s32[48]{0:T(128)S(1)} %copy-done.3, s32[1,128]{1,0:T(1,128)S(1)} %bitcast.15, s32[16,128]{1,0:T(8,128)S(1)} %get-tuple-element.7.table_ref, bf16[288,4,16,128]{3,2,1,0:T(8,128)(2,1)} %all-gather.2.cloned.1.call-done.t_ref, bf16[8,1024,128]{2,1,0:T(8,128)(2,1)S(1)} %ladder_prep.1.v_ref, ...), custom_call_target="tpu_custom_call" | custom-call | tf_op jit(solution)/shard_map/contract/pallas_call | solution.py:291
  89.2 0.0 reduce-scatter.2.cloned.1.call-update
  89.2 21.9 %reduce-scatter.2.cloned.1.call-done.z_ref = f32[12,48,128]{2,1,0:T(8,128)} async-done(((f32[48,48,128]{2,1,0:T(8,128)}), f32[12,48,128]{2,1,0:T(8,128)}) %reduce-scatter.2.cloned.1.call-update) | async-done | bytes 294928 | tf_op jit(solution)/shard_map/reduce_scatter | solution.py:357
  111.1 0.0 copy-start.1
  111.1 1.0 copy-done.1
  112.0 2.1 %expand.1 = f32[4,12,48,128]{3,2,1,0:T(8,128)S(1)} custom-call(s32[48]{0:T(128)S(1)} %copy-done.3, s32[1,128]{1,0:T(1,128)S(1)} %bitcast.16, s32[16,128]{1,0:T(8,128)S(1)} %get-tuple-element.7.table_ref, f32[12,48,128]{2,1,0:T(8,128)S(1)} %copy-done.1), custom_call_target="tpu_custom_call" | custom-call | tf_op jit(solution)/shard_map/expand/pallas_call | solution.py:340
  114.1 3.0 %copy.17 = f32[4,12,48,128]{2,0,1,3:T(4,128)} copy(f32[4,12,48,128]{3,2,1,0:T(8,128)S(1)} %expand.1) | data formatting | bytes 2359296 | tf_op jit(solution)/shard_map/expand/pallas_call | solution.py:340
  117.1 4.9 %reshape.12 = f32[32,1,9216]{2,1,0:T(1,128)S(1)} reshape(f32[128,12,4,48]{3,2,1,0:T(4,128)} %bitcast.22) | data formatting | bytes 2359296
  122.0 27.7 %all_to_all.18 = f32[32,1,9216]{2,1,0:T(1,128)S(1)} all-to-all(f32[32,1,9216]{2,1,0:T(1,128)S(1)} %reshape.12), channel_id=1, replica_groups=mesh['tile'=32,'grp'=4] {'tile'}, dimensions={0} | all-to-all | bytes 2359296 | tf_op jit(solution)/shard_map/all_to_all | solution.py:359
  149.7 0.5 broadcast
  150.3 3.6 %reduce = f32[32,9216]{1,0:T(8,128)S(1)} reduce(f32[32,1,9216]{2,1,0:T(1,128)S(1)} %all_to_all.18, f32[]{:T(128)} %broadcast), dimensions={1}, to_apply=%all_to_all.13.reduce_sub_computation | reduce | bytes 2359300 | tf_op jit(solution)/shard_map/all_to_all | solution.py:359
  153.8 4.3 %reshape.13 = f32[128,12,4,48]{3,2,1,0:T(4,128)} reshape(f32[32,9216]{1,0:T(8,128)S(1)} %reduce) | data formatting | bytes 2359296
  158.2 2.9 %copy.18 = f32[4,12,48,128]{2,3,1,0:T(8,128)S(1)} copy(f32[4,12,48,128]{2,0,1,3:T(4,128)} %bitcast.19) | data formatting | bytes 2359296 | tf_op jit(solution)/shard_map/all_to_all | solution.py:359
  161.1 3.9 %copy.19 = f32[32,4,12,48,4]{3,1,0,4,2:T(4,128)} copy(f32[32,4,12,48,4]{3,4,0,2,1:T(4,128)S(1)} %bitcast.20) | data formatting | bytes 2359296 | tf_op jit(solution)/shard_map/all_to_all | solution.py:359
  165.0 2.3 %copy.20 = f32[128,12,48,4]{0,2,1,3:T(8,128)S(1)} copy(f32[128,12,48,4]{2,0,3,1:T(8,128)} %bitcast.21) | data formatting | bytes 2359296 | tf_op jit(solution)/shard_map/all_to_all | solution.py:359
  167.4 0.1 bitcast_subtract_fusion
  167.5 1.8 %copy.21 = f32[48,12,4,128]{3,2,1,0:T(4,128)} copy(f32[48,12,4,128]{3,0,1,2:T(8,128)S(1)} %bitcast_subtract_fusion) | data formatting | bytes 2359296 | tf_op jit(solution)/shard_map/sub | solution.py:360
Async XLA Ops:
  6.5 56.1 %all-gather.2.cloned.1.call-start = ((), (), s32[]{:S(2)}) async-start(), calls=%async_computation.2 | async-start | bytes 4866048 | tf_op jit(solution)/shard_map/all_gather | solution.py:353
  6.5 1.1 copy-start
  7.6 0.7 copy-start.2
  8.3 0.7 copy-start.4
  11.9 99.2 %reduce-scatter.2.cloned.1.call-start = ((), (), s32[]{:S(2)}) async-start(), calls=%async_computation.3 | async-start | bytes 1474560 | tf_op jit(solution)/shard_map/reduce_scatter | solution.py:357
  12.0 25.6 %copy-start.5 = (s32[128]{0:T(128)S(1)}, s32[128]{0:T(128)}, u32[]{:S(2)}) copy-start(s32[128]{0:T(128)} %virt_s.1) | copy-start | bytes 1540
  12.0 25.6 %copy-start.6 = (bf16[32,128,4,128]{3,2,1,0:T(4,128)(2,1)S(1)}, bf16[32,128,4,128]{3,2,1,0:T(4,128)(2,1)}, u32[]{:S(2)}) copy-start(bf16[32,128,4,128]{3,2,1,0:T(4,128)(2,1)} %param.6) | copy-start | bytes 12582916
  37.6 25.1 %copy-start.3 = (s32[48]{0:T(128)S(1)}, s32[48]{0:T(128)}, u32[]{:S(2)}) copy-start(s32[48]{0:T(128)} %occ_s.5) | copy-start | bytes 580
  111.1 1.0 copy-start.1
Sparse Core Ops, SparseCore 0:
  12.0 50.5 all-gather.1
  89.3 21.7 reduce-scatter.1

commit v2 on v0

v2 whole, which is shorter than its diff:
```python
import jax
import jax.numpy as jnp
from jax import lax
from jax.experimental import pallas as pl
from jax.experimental.pallas import tpu as pltpu
from jax.sharding import PartitionSpec as P

NO = 48
NV = 128
SLOTS = 32
PART_C = 32
PART_A = 4
PART_J = 12
TILES = 32
GRPS = 4
ROWS = 72
TURN = 24
OWN = PART_J * TURN
SHARE = OWN // TILES
PITCH = 16
MESH = pl.DeviceIdType.MESH
IRREPS = 8
F32 = jnp.float32
BF16 = jnp.bfloat16
I32 = jnp.int32


def iota(shape, axis):
    return lax.broadcasted_iota(I32, shape, axis)


def lanes_at(values, index):
    return jnp.take_along_axis(values, index, axis=1, mode="promise_in_bounds")


def spread(selector, values):
    return jnp.dot(selector.astype(BF16), values.astype(BF16), preferred_element_type=F32).astype(I32)


def pick_rows(table, which):
    picked = jnp.broadcast_to(table[0:1], which.shape)
    for irrep in range(1, IRREPS):
        picked = jnp.where(which == irrep, jnp.broadcast_to(table[irrep : irrep + 1], which.shape), picked)
    return picked


def column_of(virt_row):
    return jnp.broadcast_to(virt_row, (NV, NV)).astype(F32).T.astype(I32)


def occupied_column(occ_s, first, rows):
    sub = iota((rows, NV), 0)
    column = jnp.zeros((rows, NV), I32)
    for i in range(rows):
        at = i if isinstance(first, int) else lax.rem(first + i, NO)
        column = jnp.where(sub == i, occ_s[at], column)
    return column


def slot_tables(virt_row):
    row = jnp.broadcast_to(virt_row, (NV, NV))
    col = column_of(virt_row)
    sub = iota((NV, NV), 0)
    lane = iota((NV, NV), 1)
    same = row == col
    rank_col = jnp.sum(jnp.where(same & (lane < sub), 1.0, 0.0), axis=1, keepdims=True)
    rank_row = jnp.sum(jnp.where(same & (sub < lane), 1.0, 0.0), axis=0, keepdims=True)
    hit = jnp.broadcast_to(rank_col, (NV, NV)).astype(I32) == lane % SLOTS
    subf = sub.astype(F32)
    entries = [
        jnp.sum(jnp.where(hit & (col == irrep), subf, 0.0), axis=0, keepdims=True)
        for irrep in range(IRREPS)
    ]
    table = jnp.concatenate(entries, axis=0).astype(I32)
    return col, table, jnp.broadcast_to(rank_row, (8, NV)).astype(I32)


def pack_rows(occ_s, t_ref, index_ref, rows_ref, out_ref, me):
    first = lax.axis_index("tile") * ROWS
    quarter = iota((8, NV), 1) // SLOTS

    def one_row(r, carry):
        pair = first + r
        irrep = occ_s[pair // NO] ^ occ_s[pair % NO]
        got = lanes_at(t_ref[r].astype(F32), index_ref[irrep])
        row = got[24:32]
        for q in (2, 1, 0):
            row = jnp.where(quarter == q, got[8 * q : 8 * q + 8], row)
        rows_ref[pl.ds(pl.multiple_of(r * 8, 8), 8)] = row
        return carry

    lax.fori_loop(0, ROWS, one_row, 0, unroll=8)
    for block in range(ROWS // 8):
        for half in range(4):
            pair_of = [
                rows_ref[pl.ds(block * 64 + 2 * half + odd, 8, stride=8)] for odd in range(2)
            ]
            out_ref[me, half, block] = jnp.concatenate(pair_of, axis=0).astype(BF16)


class Ring:
    def __init__(self, t_all, send_sem, recv_sem):
        tile = lax.axis_index("tile")
        self.at = (tile // 8, (tile // 2) % 4, tile % 2)
        self.buffer, self.send_sem, self.recv_sem = t_all, send_sem, recv_sem
        self.named = {}
        self.started = []

    def tile_of(self, dx, dz, core):
        x, z, _ = self.at
        return ((x + dx + 4) % 4 * 4 + (z + dz + 4) % 4) * 2 + core

    def copy(self, name, origin, parts, target, core_of):
        number = self.named.setdefault(name, len(self.named))
        block = self.buffer.at[self.tile_of(origin[0], origin[1], core_of), parts[0] : parts[1]]
        return pltpu.make_async_remote_copy(
            src_ref=block,
            dst_ref=block,
            send_sem=self.send_sem.at[number],
            recv_sem=self.recv_sem.at[number],
            device_id={"tile": target},
            device_id_type=MESH,
        )

    def send(self, name, origin, parts, step):
        core = self.at[2]
        if step is None:
            copy = self.copy(name, origin, parts, self.tile_of(0, 0, 1 - core), core)
        else:
            copy = self.copy(name, origin, parts, self.tile_of(step[0], step[1], core), core)
        copy.start()
        self.started.append(copy)

    def arrive(self, name, origin, parts, core_of=None):
        core = self.at[2]
        self.copy(name, origin, parts, self.tile_of(0, 0, 1 - core), core if core_of is None else core_of).wait_recv()


def gather_steps(ring):
    def place(family, first, second):
        return (first, second) if family == 0 else (second, first)

    def both(family):
        return (2 * family, 2 * family + 2)

    def part(family, which):
        return (2 * family + which, 2 * family + which + 1)

    def begin():
        for family in range(2):
            ring.send((family, "f", 1), (0, 0), both(family), place(family, 1, 0))
            ring.send((family, "f", -1), (0, 0), both(family), place(family, -1, 0))
        for family in range(2):
            for step in (1, -1):
                ring.send((family, "s", 0, step), (0, 0), both(family), place(family, 0, step))
        for family in range(2):
            ring.send((family, "c", 0, 0), (0, 0), both(family), None)

    def spread_first(family, k):
        for step in (1, -1):
            ring.send((family, "s", k, step), place(family, k, 0), both(family), place(family, 0, step))
        ring.send((family, "c", k, 0), place(family, k, 0), both(family), None)

    def near():
        for family in range(2):
            for step in (1, -1):
                origin = place(family, -step, 0)
                ring.arrive((family, "f", step), origin, both(family))
                ring.send((family, "g", step), origin, part(family, 0 if step == 1 else 1), place(family, step, 0))
        for family in range(2):
            for k in (-1, 1):
                spread_first(family, k)

    def far():
        for family in range(2):
            for step in (1, -1):
                ring.arrive((family, "g", step), place(family, 2, 0), part(family, 0 if step == 1 else 1))
            spread_first(family, 2)

    def second(k):
        def run():
            for family in range(2):
                for step in (1, -1):
                    origin = place(family, k, -step)
                    ring.arrive((family, "s", k, step), origin, both(family))
                    ring.send((family, "t", k, step), origin, part(family, 0 if step == 1 else 1), place(family, 0, step))
                    ring.send((family, "c", k, -step), origin, both(family), None)

        return run

    def last(k):
        def run():
            for family in range(2):
                for step in (1, -1):
                    ring.arrive((family, "t", k, step), place(family, k, 2), part(family, 0 if step == 1 else 1))
                ring.send((family, "c", k, 2), place(family, k, 2), both(family), None)

        return run

    def siblings():
        for family in range(2):
            for k in (0, -1, 1, 2):
                for m in (0, -1, 1, 2):
                    ring.arrive((family, "c", k, m), place(family, k, m), both(family), 1 - ring.at[2])

    def settle():
        for copy in ring.started:
            copy.wait_send()

    ks = (0, -1, 1, 2)
    return [begin, near, far] + [second(k) for k in ks] + [last(k) for k in ks] + [siblings, settle]


TRANSFERS = 72
C_STEP = 4
KC = NO * PART_C
JP = NO // 2
JP_STEP = 4


def contract_body(
    occ_s, virt_s, virt_ref, t_ref, v_hbm, w_hbm, out_ref, table_ref,
    t_all, w_all, v_all, v_sem, w_sem, send_sem, recv_sem,
    index_ref, column_ref, rows_ref, v_index_ref, perm_ref, sorted_ref, right_ref,
    ladder_ref, cut_ref, left_ref, c_index_ref, total_ref,
):
    wide = NV * PART_A
    tile = lax.axis_index("tile")
    first_a = tile * PART_A
    first_c = lax.axis_index("grp") * PART_C
    v_copies = [
        pltpu.make_async_copy(v_hbm.at[pl.ds(C_STEP * n, C_STEP)], v_all.at[pl.ds(C_STEP * n, C_STEP)], v_sem.at[n])
        for n in range(PART_C // C_STEP)
    ]
    w_copies = [pltpu.make_async_copy(w_hbm.at[:, n], w_all.at[n], w_sem.at[n]) for n in range(JP)]
    for copy in v_copies + w_copies:
        copy.start()

    ring = Ring(t_all, send_sem, recv_sem)
    steps = gather_steps(ring)
    core = ring.at[2]
    barrier = pltpu.get_barrier_semaphore()
    for target in (
        ring.tile_of(1, 0, core), ring.tile_of(-1, 0, core), ring.tile_of(0, 1, core),
        ring.tile_of(0, -1, core), ring.tile_of(0, 0, 1 - core),
    ):
        pl.semaphore_signal(barrier, inc=1, device_id={"tile": target}, device_id_type=MESH)

    col, table, rank = slot_tables(virt_ref[...])
    column_ref[...] = col
    table_ref[0:8] = table
    table_ref[8:16] = rank
    c_col = column_ref[pl.ds(pl.multiple_of(first_c, PART_C), PART_C)]
    for irrep in range(IRREPS):
        index_ref[irrep] = pick_rows(table, c_col ^ irrep)
    pack_rows(occ_s, t_ref, index_ref, rows_ref, t_all, tile)
    pl.semaphore_wait(barrier, 5)
    steps[0]()

    sub = iota((wide, NV), 0)
    lane = iota((wide, NV), 1)
    of_d = spread(lane == sub // PART_A, col)
    of_a = spread(lane == first_a + sub % PART_A, col)
    both_irreps = of_d ^ of_a
    for irrep in range(IRREPS):
        v_index_ref[irrep] = pick_rows(table, both_irreps ^ irrep)
    repeat = iota((NV, wide), 1) // PART_A == iota((NV, wide), 0)
    virt8 = jnp.broadcast_to(virt_ref[...], (8, NV))
    irrep_row = spread(virt8, repeat)[0:1]
    rank_row = spread(rank, repeat)[0:1]
    at = iota((IRREPS * SLOTS, wide), 0)
    perm_ref[...] = jnp.where((irrep_row == at // SLOTS) & (rank_row == at % SLOTS), 1.0, 0.0).astype(BF16)
    steps[1]()

    def prep(c, carry):
        own = iota((wide, NV), 1) // SLOTS == iota((wide, NV), 0) % PART_A
        irrep_c = virt_s[first_c + c]
        got = lanes_at(v_all[c].astype(F32), v_index_ref[irrep_c])
        compact = jnp.where(own, got, 0.0).astype(BF16)
        ordered = jnp.dot(perm_ref[...], compact, preferred_element_type=F32).astype(BF16)
        sorted_ref[...] = ordered.reshape(IRREPS, SLOTS, NV)
        start = pl.multiple_of((c % 8) * NV + (c // 8) * SLOTS, SLOTS)
        for irrep in range(IRREPS):
            right_ref[irrep // 2, pl.ds(start, SLOTS), (irrep % 2) * NV : (irrep % 2 + 1) * NV] = sorted_ref[irrep_c ^ irrep]
        return carry

    for n in range(PART_C // C_STEP):
        v_copies[n].wait()
        lax.fori_loop(C_STEP * n, C_STEP * (n + 1), prep, 0)
        steps[2 + n]()

    occ_col = occupied_column(occ_s, 0, NO)
    subd = iota((NV, 2 * NV), 0)
    laned = iota((NV, 2 * NV), 1)
    of_a2 = subd == first_a + laned // (2 * PART_C)
    of_c2 = subd == first_c + (laned // 2) % PART_C
    a_irrep = spread(virt8, of_a2)
    ac_irrep = (a_irrep ^ spread(virt8, of_c2))[0:1]
    a_rank = spread(rank, of_a2)[0:1]
    deep = (PART_C * SLOTS, 2 * NV)
    row_at = iota(deep, 0)
    lane_at = iota(deep, 1)
    c_at = 8 * ((row_at % NV) // SLOTS) + row_at // NV
    wanted = (c_at == (lane_at // 2) % PART_C) & (lane_at % 2 == 0) & (a_rank == row_at % SLOTS)
    cut = jnp.where(wanted, 1.0, 0.0).astype(BF16)
    for a in range(PART_A):
        base = occ_col ^ a_irrep[0:1, 2 * a * PART_C : 2 * a * PART_C + 1]
        for irrep in range(IRREPS):
            c_index_ref[irrep, a * NO : (a + 1) * NO] = pick_rows(table, base ^ irrep)
    for n in range(2 + PART_C // C_STEP, len(steps) - 1):
        steps[n]()

    chips = 4
    m_rows = chips * 2 * ROWS

    def ladder_block(n, carry):
        got = t_all[pl.ds(n * 2 * chips, 2 * chips)].astype(F32)
        planes = [
            got[:, m // 2, :, (m % 2) * 8 : (m % 2) * 8 + 8].reshape(m_rows, NV).astype(BF16)
            for m in range(8)
        ]
        left = jnp.concatenate(planes, axis=1)
        pair_irrep = jnp.concatenate([occ_col ^ occ_s[n * (m_rows // NO) + u] for u in range(m_rows // NO)], axis=0)
        total = jnp.zeros((m_rows, NV), F32)
        for pair in range(4):
            both = jnp.dot(left, right_ref[pair], preferred_element_type=F32)
            total = jnp.where(pair_irrep == 2 * pair, both[:, :NV], total)
            total = jnp.where(pair_irrep == 2 * pair + 1, both[:, NV:], total)
        rows = pl.ds(pl.multiple_of(n * m_rows, m_rows), m_rows)
        ladder_ref[rows] = total
        piece = jnp.dot(left, cut, preferred_element_type=F32)
        for half in range(2):
            lanes = slice(half * NV, (half + 1) * NV)
            cut_ref[half, rows] = jnp.where(pair_irrep == ac_irrep[:, lanes], piece[:, lanes], 0.0)
        return carry

    lax.fori_loop(0, 16 // chips, ladder_block, 0)

    lane48 = iota((NO, NV), 1)
    odd_half = lane48 // (2 * PART_C) == 1

    def left_block(chunk, carry):
        for half in range(2):
            lower = cut_ref[half, pl.ds(2 * chunk, NO, stride=NO)]
            upper = cut_ref[half, pl.ds(2 * chunk + 1, NO, stride=NO)]
            even_a = jnp.where(odd_half, pltpu.roll(upper, 2 * PART_C, 1), lower)
            odd_a = jnp.where(odd_half, upper, pltpu.roll(lower, 2 * PART_C, 1))
            for odd, piece in enumerate((even_a, odd_a)):
                a = 2 * half + odd
                lanes = pl.ds(pl.multiple_of(chunk * NV, NV), NV)
                left_ref[a * NO : (a + 1) * NO, lanes] = piece.astype(BF16)
                left_ref[(PART_A + a) * NO : (PART_A + a + 1) * NO, lanes] = pltpu.roll(piece, 1, 1).astype(BF16)
        return carry

    lax.fori_loop(0, JP, left_block, 0, unroll=2)

    flat = w_all.reshape(JP * 2 * KC, NV)
    span = 2 * NO
    for copy in w_copies:
        copy.wait()

    def cycle_block(n, carry):
        right = jnp.concatenate(
            [flat[pl.ds(pl.multiple_of((n * JP_STEP + u) * 2 * KC, 2 * KC), 2 * KC)] for u in range(JP_STEP)], axis=1
        )
        both = jnp.dot(left_ref[...], right, preferred_element_type=F32)
        for u in range(JP_STEP):
            for odd in range(2):
                j = (n * JP_STEP + u) * 2 + odd
                rows = both[odd * PART_A * NO : (odd + 1) * PART_A * NO, u * NV : (u + 1) * NV]
                got = lanes_at(rows, c_index_ref[occ_s[j]])
                value = got[3 * NO :]
                for a in (2, 1, 0):
                    value = jnp.where(lane48 // SLOTS == a, got[a * NO : (a + 1) * NO], value)
                value = value + 0.5 * ladder_ref[pl.ds(j, NO, stride=NO)]
                start = pl.multiple_of(j * span, NO)
                total_ref[pl.ds(start, NO)] = value
                total_ref[pl.ds(start + NO, NO)] = value
        return carry

    lax.fori_loop(0, JP // JP_STEP, cycle_block, 0)
    total_ref[pl.ds(NO * span, TURN * span)] = total_ref[pl.ds(0, TURN * span)]

    def anti(j, carry):
        ahead = total_ref[pl.ds(j * span + j + 1, TURN, stride=1)]
        across = total_ref[pl.ds((j + 1) * span + j, TURN, stride=span)]
        out_ref[j] = ahead - across
        return carry

    lax.fori_loop(0, NO, anti, 0, unroll=4)
    steps[-1]()


def contract(occ, virt, virt_row, amplitudes, ladder_rows, cycle_pairs):
    wide = NV * PART_A
    pairs = NO * NO
    vmem = pl.BlockSpec(memory_space=pltpu.VMEM)
    smem = pl.BlockSpec(memory_space=pltpu.SMEM)
    hbm = pl.BlockSpec(memory_space=pl.ANY)
    return pl.pallas_call(
        contract_body,
        out_shape=(
            jax.ShapeDtypeStruct((NO, TURN, NV), F32),
            jax.ShapeDtypeStruct((16, NV), I32),
        ),
        in_specs=[smem, smem, vmem, vmem, hbm, hbm],
        out_specs=(vmem, vmem),
        scratch_shapes=[
            pltpu.VMEM((TILES, 4, ROWS // 8, 16, NV), BF16),
            pltpu.VMEM((JP, KC, 2, NV), BF16),
            pltpu.VMEM((PART_C, wide, NV), BF16),
            pltpu.SemaphoreType.DMA((PART_C // C_STEP,)),
            pltpu.SemaphoreType.DMA((JP,)),
            pltpu.SemaphoreType.DMA((TRANSFERS,)),
            pltpu.SemaphoreType.DMA((TRANSFERS,)),
            pltpu.VMEM((IRREPS, PART_C, NV), I32),
            pltpu.VMEM((NV, NV), I32),
            pltpu.VMEM((ROWS * 8, NV), F32),
            pltpu.VMEM((IRREPS, wide, NV), I32),
            pltpu.VMEM((IRREPS * SLOTS, wide), BF16),
            pltpu.VMEM((IRREPS, SLOTS, NV), BF16),
            pltpu.VMEM((4, PART_C * SLOTS, 2 * NV), BF16),
            pltpu.VMEM((pairs, NV), F32),
            pltpu.VMEM((2, pairs, NV), F32),
            pltpu.VMEM((2 * PART_A * NO, 2 * KC), BF16),
            pltpu.VMEM((IRREPS, PART_A * NO, NV), I32),
            pltpu.VMEM(((NO + TURN) * 2 * NO, NV), F32),
        ],
        compiler_params=pltpu.CompilerParams(
            vmem_limit_bytes=60 * 2**20, collective_id=0, has_side_effects=True
        ),
        name="contract",
    )(occ, virt, virt_row, amplitudes, ladder_rows, cycle_pairs)


def exchange_body(
    occ_s, virt_ref, table_ref, z_ref, own_ref, near_ref, far_ref,
    stage_ref, direct_ref, merged_ref, first_ref, first_in, second_ref, second_in,
    index_ref, near_out, far_out, sum_send, sum_recv, a_send, a_recv, b_send, b_recv, f_send, f_recv,
):
    tile = lax.axis_index("tile")
    grp = lax.axis_index("grp")
    up, down, over = (grp + 1) % GRPS, (grp + 3) % GRPS, (grp + 2) % GRPS
    barrier = pltpu.get_barrier_semaphore()
    for target in (up, down, over):
        pl.semaphore_signal(barrier, inc=1, device_id={"grp": target}, device_id_type=MESH)
    for d in range(1, TILES):
        pl.semaphore_signal(barrier, inc=1, device_id={"tile": (tile + d) % TILES}, device_id_type=MESH)
    pl.semaphore_wait(barrier, TILES + 2)

    half = PART_J // 2

    def block(owner, part):
        return pl.ds(owner * PART_J + part * half, half)

    def to(axis, target, src, dst, send, recv):
        return pltpu.make_async_remote_copy(
            src_ref=src, dst_ref=dst, send_sem=send, recv_sem=recv,
            device_id={axis: target}, device_id_type=MESH,
        )

    sends = [
        to("grp", up, z_ref.at[block(over, 0)], stage_ref.at[0], sum_send.at[0], sum_recv.at[0]),
        to("grp", down, z_ref.at[block(over, 1)], stage_ref.at[1], sum_send.at[1], sum_recv.at[1]),
        to("grp", up, z_ref.at[block(up, 1)], direct_ref.at[0], sum_send.at[2], sum_recv.at[2]),
        to("grp", down, z_ref.at[block(down, 0)], direct_ref.at[1], sum_send.at[3], sum_recv.at[3]),
        to("grp", up, merged_ref.at[0], direct_ref.at[2], sum_send.at[4], sum_recv.at[4]),
        to("grp", down, merged_ref.at[1], direct_ref.at[3], sum_send.at[5], sum_recv.at[5]),
    ]
    for copy in sends[:4]:
        copy.start()

    table = table_ref[0:8]
    sub = iota((NV, NV), 0)
    lane = iota((NV, NV), 1)
    turned = sub == 4 * (lane % SLOTS) + lane // SLOTS
    rank_turned = spread(table_ref[8:16], turned)[0:1]
    irrep_turned = spread(jnp.broadcast_to(virt_ref[...], (8, NV)), turned)[0:1]
    irrep_col = column_of(irrep_turned)
    table_turned = (table % 4) * SLOTS + table // 4
    for irrep in range(IRREPS):
        index_ref[irrep] = pick_rows(table_turned, irrep_col ^ irrep)

    sends[0].wait_recv()
    merged_ref[0] = stage_ref[0] + z_ref[block(up, 0)]
    sends[4].start()
    sends[1].wait_recv()
    merged_ref[1] = stage_ref[1] + z_ref[block(down, 1)]
    sends[5].start()
    sends[2].wait_recv()
    sends[3].wait_recv()
    sends[4].wait_recv()
    sends[5].wait_recv()
    lower = z_ref[block(grp, 0)] + direct_ref[1] + direct_ref[2]
    upper = z_ref[block(grp, 1)] + direct_ref[0] + direct_ref[3]
    own_ref[0 : OWN // 2] = lower.reshape(OWN // 2, NV)
    own_ref[OWN // 2 : OWN] = upper.reshape(OWN // 2, NV)
    for u in range(TILES):
        first_ref[u] = own_ref[u * SHARE : (u + 1) * SHARE]

    def swap_all(src, dst, send, recv):
        copies = []
        for d in range(1, TILES):
            target = (tile + d) % TILES
            copy = to("tile", target, src.at[target], dst.at[pl.ds(pl.multiple_of(tile * PITCH, PITCH), SHARE)], send.at[d], recv.at[d])
            copy.start()
            copies.append(copy)
        return copies

    first_in[pl.ds(pl.multiple_of(tile * PITCH, PITCH), SHARE)] = first_ref[tile]
    copies = swap_all(first_ref, first_in, a_send, a_recv)
    for copy in copies:
        copy.wait_recv()

    quarter = iota((TILES, NV), 1) // SLOTS

    def one(n, carry):
        row = tile * SHARE + n
        j = grp * PART_J + row // TURN
        i = (j + row % TURN + 1) % NO
        irrep = occ_s[i] ^ occ_s[j]
        rows = first_in[pl.ds(n, TILES, stride=PITCH)]
        full = jnp.concatenate(
            [lanes_at(rows, jnp.broadcast_to(rank_turned + a * SLOTS, (TILES, NV))) for a in range(PART_A)], axis=0
        )
        anti = full - full.T
        got = lanes_at(anti, index_ref[irrep])
        value = got[3 * TILES :]
        for a in (2, 1, 0):
            value = jnp.where(quarter == a, got[a * TILES : (a + 1) * TILES], value)
        for t in range(TILES):
            second_ref[t, pl.ds(n, 1)] = value[t : t + 1]
        return carry

    lax.fori_loop(0, SHARE, one, 0)
    second_in[pl.ds(pl.multiple_of(tile * PITCH, PITCH), SHARE)] = second_ref[tile]
    more = swap_all(second_ref, second_in, b_send, b_recv)
    for copy in more:
        copy.wait_recv()
    for u in range(TILES):
        own_ref[u * SHARE : (u + 1) * SHARE] = second_in[u * PITCH : u * PITCH + SHARE]
    for x in range(PART_J):
        near_out[x * PART_J : (x + 1) * PART_J] = own_ref[x * TURN + 11 - x : x * TURN + 23 - x]
        far_out[x * PART_J : (x + 1) * PART_J] = own_ref[x * TURN + 23 - x : x * TURN + 35 - x]
    ends = [
        to("grp", up, near_out, near_ref, f_send.at[0], f_recv.at[0]),
        to("grp", over, far_out, far_ref, f_send.at[1], f_recv.at[1]),
    ]
    for copy in ends:
        copy.start()
    for copy in sends + copies + more:
        copy.wait_send()
    for copy in ends:
        copy.wait()


def exchange(occ, virt_row, table, partial_sum):
    vmem = pl.BlockSpec(memory_space=pltpu.VMEM)
    smem = pl.BlockSpec(memory_space=pltpu.SMEM)
    block = PART_J * PART_J
    half = (PART_J // 2, TURN, NV)
    return pl.pallas_call(
        exchange_body,
        out_shape=(
            jax.ShapeDtypeStruct((OWN, NV), F32),
            jax.ShapeDtypeStruct((block, NV), F32),
            jax.ShapeDtypeStruct((block, NV), F32),
        ),
        in_specs=[smem, vmem, vmem, vmem],
        out_specs=(vmem, vmem, vmem),
        scratch_shapes=[
            pltpu.VMEM((2,) + half, F32),
            pltpu.VMEM((4,) + half, F32),
            pltpu.VMEM((2,) + half, F32),
            pltpu.VMEM((TILES, SHARE, NV), F32),
            pltpu.VMEM((TILES * PITCH, NV), F32),
            pltpu.VMEM((TILES, SHARE, NV), F32),
            pltpu.VMEM((TILES * PITCH, NV), F32),
            pltpu.VMEM((IRREPS, NV, NV), I32),
            pltpu.VMEM((block, NV), F32),
            pltpu.VMEM((block, NV), F32),
            pltpu.SemaphoreType.DMA((6,)),
            pltpu.SemaphoreType.DMA((6,)),
            pltpu.SemaphoreType.DMA((TILES,)),
            pltpu.SemaphoreType.DMA((TILES,)),
            pltpu.SemaphoreType.DMA((TILES,)),
            pltpu.SemaphoreType.DMA((TILES,)),
            pltpu.SemaphoreType.DMA((2,)),
            pltpu.SemaphoreType.DMA((2,)),
        ],
        compiler_params=pltpu.CompilerParams(
            vmem_limit_bytes=32 * 2**20, collective_id=1, has_side_effects=True
        ),
        name="exchange",
    )(occ, virt_row, table, partial_sum)


def expand_body(occ_s, virt_ref, table_ref, own_ref, near_ref, far_ref, out_ref, rows_ref):
    first_a = lax.axis_index("tile") * PART_A
    grp = lax.axis_index("grp")
    first_j = grp * PART_J
    occ_col = occupied_column(occ_s, first_j, NO)
    virt_row = jnp.broadcast_to(virt_ref[...], (NO, NV))
    rank_row = jnp.broadcast_to(table_ref[8:9], (NO, NV))
    virt8 = jnp.broadcast_to(virt_ref[...], (8, NV))
    a_irrep = spread(virt8, iota((NV, NV), 0) == first_a + iota((NV, NV), 1) // PART_C)
    n = PART_J
    for x in range(n):
        at = rows_ref.at[x]
        at[x : x + 1] = jnp.zeros((1, NV), F32)
        if x < n - 1:
            at[x + 1 : n] = own_ref[x * TURN : x * TURN + n - 1 - x]
        if x > 0:
            at[0:x] = -own_ref[pl.ds(x - 1, x, stride=TURN - 1)]
        at[n : 2 * n] = own_ref[x * TURN + 11 - x : x * TURN + 23 - x]
        at[2 * n : 2 * n + x + 1] = own_ref[x * TURN + 23 - x : x * TURN + 24]
        if x < n - 1:
            at[2 * n + x + 1 : 3 * n] = -far_ref[pl.ds((x + 1) * n + x, n - 1 - x, stride=n)]
        at[3 * n : 4 * n] = -near_ref[pl.ds(x, n, stride=n)]
    for x in range(n):
        rows = rows_ref[x]
        irrep_j = occ_s[first_j + x]
        for a in range(PART_A):
            got = lanes_at(rows, rank_row + a * SLOTS)
            want = virt_row ^ a_irrep[0:1, a * PART_C : a * PART_C + 1] ^ irrep_j
            value = jnp.where(occ_col == want, got, 0.0)
            for b in range(GRPS):
                start = lax.rem(grp + b, GRPS) * (n * n * PART_A) + x * PART_A + a
                out_ref[pl.ds(start, n, stride=n * PART_A)] = value[b * n : (b + 1) * n]


def expand(occ, virt_row, table, own, near, far):
    vmem = pl.BlockSpec(memory_space=pltpu.VMEM)
    return pl.pallas_call(
        expand_body,
        out_shape=jax.ShapeDtypeStruct((NO * PART_J * PART_A, NV), F32),
        in_specs=[pl.BlockSpec(memory_space=pltpu.SMEM)] + [vmem] * 5,
        out_specs=vmem,
        scratch_shapes=[pltpu.VMEM((PART_J, NO, NV), F32)],
        compiler_params=pltpu.CompilerParams(vmem_limit_bytes=32 * 2**20),
        name="expand",
    )(occ, virt_row, table, own, near, far)


def shards(amplitudes, ladder_ints, cycle_ints, occ_irrep, virt_irrep):
    virt_row = virt_irrep.reshape(1, NV)
    partial_sum, table = contract(
        occ_irrep, virt_irrep, virt_row, amplitudes,
        ladder_ints.reshape(PART_C, NV * PART_A, NV), cycle_ints.reshape(KC, JP, 2, NV),
    )
    own, near, far = exchange(occ_irrep, virt_row, table, partial_sum)
    return expand(occ_irrep, virt_row, table, own, near, far).reshape(NO, PART_J, PART_A, NV)


def solution(mesh):
    placed = (
        P("tile", "grp", None),
        P("grp", None, "tile", None),
        P(None, "grp", None, None),
        P(),
        P(),
    )
    return jax.shard_map(
        shards, mesh=mesh, in_specs=placed, out_specs=P(None, "grp", "tile", None), check_vma=False
    )
```

time: 377 us -> 94.3 us (0.25); the launches traced: 372 us -> 94.1 us
  waiting for transfers between devices: 152 us -> 0 us
  local copies, waits for them, and re-layouts: 120 us -> 1.76 us
  Pallas kernels: 0 us -> 92.3 us
  matrix products: 61.8 us -> 0 us
  between operations: 13.7 us -> 0.04 us
  other arithmetic: 12.5 us -> 0 us
  starting transfers between devices: 12.2 us -> 0 us
    pallas_call x0 -> x3, Pallas kernels: none -> 92.3 us  [the longest x1 56.5 us: contract(): pl.pallas_call(contract_body, out_shape=(jax.ShapeDtypeStruct((NO, TURN,...]
    all_gather x1 -> x0, waiting for transfers between devices: 70.1 us -> none  [shards(): gathered = lax.all_gather(masked, 'tile', axis=0, tiled=True)]
    dot_general x2 -> x0, matrix products: 61.8 us -> none  [the longest x1 45.3 us: shards(): jnp.einsum('ikca,kcjb->ijab', cycle_slice.reshape(occ, occ, part_c, part_...]
    reduce_scatter x1 -> x0, waiting for transfers between devices: 50.3 us -> none  [shards(): lax.psum_scatter(partial_value, 'grp', scatter_dimension=1, tiled=True)]
    dot_general x2 -> x0, local copies, waits for them, and re-layouts: 34.7 us -> none  [shards(): jnp.dot(gathered.reshape(gathered.shape[0], part_c * virt), ladder_flat,...]
    all_to_all x2 -> x0, waiting for transfers between devices: 31.2 us -> none  [the longest x1 16.1 us: shards(): lax.all_to_all(anti, 'grp', split_axis=0, concat_axis=1, tiled=True)]
    reshape x1 -> x0, local copies, waits for them, and re-layouts: 23 us -> none  [shards(): cycle_slice.reshape(occ, occ, part_c, part_a)]
    dynamic_slice x4 -> x0, local copies, waits for them, and re-layouts: 19.5 us -> none  [the longest x1 18.6 us: shards(): lax.dynamic_slice_in_dim(gathered, tile_at * part_a, part_a, 2)]
  transfers between devices with their start and end apart: 4 -> 0, of which waited for: 4 -> 0; matrix products, arithmetic and copies ran while one was open for 4% -> 0% of each run, Pallas kernels for 0% -> 0%
where the time goes in v2:
time: 94.3 us; the launch traced here: 94.1 us
  Pallas kernels  92.3 us (98%)
  local copies, waits for them, and re-layouts  1.76 us (2%)
    pallas_call x1, Pallas kernels, contract(): pl.pallas_call(contract_body, out_shape=(jax.ShapeDtypeStruct((NO, TURN,...  56.5 us
    pallas_call x1, Pallas kernels, exchange(): pl.pallas_call(exchange_body, out_shape=(jax.ShapeDtypeStruct((OWN, NV),...  33.5 us
    pallas_call x1, Pallas kernels, expand(): pl.pallas_call(expand_body, out_shape=jax.ShapeDtypeStruct((NO * PART_J *...  2.37 us

profile of v2, /device:TPU:1, one launch (start us, length us, event | category | flops | bytes accessed | tf_op | source)
XLA Modules:
  0.0 94.1 jit_solution(15166061577197546508)
XLA Ops:
  0.0 0.0 copy-start.2
  0.0 0.0 copy-start.3
  0.0 56.5 %contract.1 = (f32[48,24,128]{2,1,0:T(8,128)}, s32[16,128]{1,0:T(8,128)}) custom-call(s32[48]{0:T(128)} %occ_s.5, s32[128]{0:T(128)} %virt_s.1, s32[1,128]{1,0:T(1,128)} %bitcast.4, bf16[72,32,128]{2,1,0:T(8,128)(2,1)} %t_ref.1, bf16[32,512,128]{2,1,0:T(8,128)(2,1)} %bitcast.8, bf16[1536,24,2,128]{3,2,1,0:T(2,128)(2,1)} %bitcast.7), custom_call_target="tpu_custom_call" | custom-call | tf_op jit(solution)/shard_map/contract/pallas_call | solution.py:400
  56.5 0.0 copy-done.2
  56.5 0.0 copy-done.3
  56.5 0.0 copy-start
  56.5 1.1 %copy-done = f32[48,24,128]{2,1,0:T(8,128)S(1)} copy-done((f32[48,24,128]{2,1,0:T(8,128)S(1)}, f32[48,24,128]{2,1,0:T(8,128)}, u32[]{:S(2)}) %copy-start) | copy-done | bytes 589848
  57.6 0.0 copy-start.1
  57.6 0.7 copy-done.1
  58.3 33.5 %exchange.1 = (f32[288,128]{1,0:T(8,128)S(1)}, f32[144,128]{1,0:T(8,128)S(1)}, f32[144,128]{1,0:T(8,128)S(1)}) custom-call(s32[48]{0:T(128)S(1)} %copy-done.3, s32[1,128]{1,0:T(1,128)S(1)} %bitcast.5, s32[16,128]{1,0:T(8,128)S(1)} %copy-done.1, f32[48,24,128]{2,1,0:T(8,128)S(1)} %copy-done), custom_call_target="tpu_custom_call" | custom-call | tf_op jit(solution)/shard_map/exchange/pallas_call | solution.py:562
  91.7 2.4 %expand.1 = f32[2304,128]{1,0:T(8,128)} custom-call(s32[48]{0:T(128)S(1)} %copy-done.3, s32[1,128]{1,0:T(1,128)S(1)} %bitcast.6, s32[16,128]{1,0:T(8,128)S(1)} %copy-done.1, f32[288,128]{1,0:T(8,128)S(1)} %get-tuple-element.12.own_ref, f32[144,128]{1,0:T(8,128)S(1)} %get-tuple-element.13.near_ref, f32[144,128]{1,0:T(8,128)S(1)} %get-tuple-element.14.far_ref), custom_call_target="tpu_custom_call" | custom-call | tf_op jit(solution)/shard_map/expand/pallas_call | solution.py:634
Async XLA Ops:
  0.0 56.5 %copy-start.2 = (s32[128]{0:T(128)S(1)}, s32[128]{0:T(128)}, u32[]{:S(2)}) copy-start(s32[128]{0:T(128)} %virt_s.1) | copy-start | bytes 1540
  0.0 56.5 %copy-start.3 = (s32[48]{0:T(128)S(1)}, s32[48]{0:T(128)}, u32[]{:S(2)}) copy-start(s32[48]{0:T(128)} %occ_s.5) | copy-start | bytes 580
  56.5 1.1 %copy-start = (f32[48,24,128]{2,1,0:T(8,128)S(1)}, f32[48,24,128]{2,1,0:T(8,128)}, u32[]{:S(2)}) copy-start(f32[48,24,128]{2,1,0:T(8,128)} %get-tuple-element.11.z_ref) | copy-start | bytes 1769476
  57.6 0.7 copy-start.1

commit v3 on v2

--- a/solution.py
+++ b/solution.py
@@ -72,7 +72,8 @@
         for irrep in range(IRREPS)
     ]
     table = jnp.concatenate(entries, axis=0).astype(I32)
-    return col, table, jnp.broadcast_to(rank_row, (8, NV)).astype(I32)
+    rank_col = jnp.broadcast_to(rank_col, (NV, NV)).astype(I32)
+    return col, table, jnp.broadcast_to(rank_row, (8, NV)).astype(I32), rank_col
 
 
 def pack_rows(occ_s, t_ref, index_ref, rows_ref, out_ref, me):
@@ -197,41 +198,40 @@
 
         return run
 
-    def siblings():
+    def sibling(origin):
         for family in range(2):
-            for k in (0, -1, 1, 2):
-                for m in (0, -1, 1, 2):
-                    ring.arrive((family, "c", k, m), place(family, k, m), both(family), 1 - ring.at[2])
+            k, m = place(family, origin[0], origin[1])
+            ring.arrive((family, "c", k, m), origin, both(family), 1 - ring.at[2])
 
     def settle():
         for copy in ring.started:
             copy.wait_send()
 
-    ks = (0, -1, 1, 2)
-    return [begin, near, far] + [second(k) for k in ks] + [last(k) for k in ks] + [siblings, settle]
+    steps = {"begin": begin, "near": near, "far": far, "sibling": sibling, "settle": settle}
+    for k in (0, -1, 1, 2):
+        steps["second", k] = second(k)
+        steps["last", k] = last(k)
+    return steps
 
 
 TRANSFERS = 72
-C_STEP = 4
 KC = NO * PART_C
 JP = NO // 2
 JP_STEP = 4
+FAR = 72
 
 
 def contract_body(
-    occ_s, virt_s, virt_ref, t_ref, v_hbm, w_hbm, out_ref, table_ref,
+    occ_s, virt_s, virt_ref, t_ref, v_hbm, w_hbm, own_ref, near_ref, far_ref, table_ref,
     t_all, w_all, v_all, v_sem, w_sem, send_sem, recv_sem,
-    index_ref, column_ref, rows_ref, v_index_ref, perm_ref, sorted_ref, right_ref,
-    ladder_ref, cut_ref, left_ref, c_index_ref, total_ref,
+    index_ref, column_ref, rows_ref, perm_ref, x_all, slot_ref, right_ref, cut_one_ref,
+    ladder_ref, cut_ref, left_ref, c_index_ref, total_ref, both_a, both_b, z_ref, *exchange_refs,
 ):
-    wide = NV * PART_A
     tile = lax.axis_index("tile")
+    grp = lax.axis_index("grp")
     first_a = tile * PART_A
-    first_c = lax.axis_index("grp") * PART_C
-    v_copies = [
-        pltpu.make_async_copy(v_hbm.at[pl.ds(C_STEP * n, C_STEP)], v_all.at[pl.ds(C_STEP * n, C_STEP)], v_sem.at[n])
-        for n in range(PART_C // C_STEP)
-    ]
+    first_c = grp * PART_C
+    v_copies = [pltpu.make_async_copy(v_hbm.at[:, :, n], v_all.at[n], v_sem.at[n]) for n in range(2)]
     w_copies = [pltpu.make_async_copy(w_hbm.at[:, n], w_all.at[n], w_sem.at[n]) for n in range(JP)]
     for copy in v_copies + w_copies:
         copy.start()
@@ -245,8 +245,10 @@
         ring.tile_of(0, -1, core), ring.tile_of(0, 0, 1 - core),
     ):
         pl.semaphore_signal(barrier, inc=1, device_id={"tile": target}, device_id_type=MESH)
-
-    col, table, rank = slot_tables(virt_ref[...])
+    for d in range(1, GRPS):
+        pl.semaphore_signal(barrier, inc=1, device_id={"grp": (grp + d) % GRPS}, device_id_type=MESH)
+
+    col, table, rank, rank_col = slot_tables(virt_ref[...])
     column_ref[...] = col
     table_ref[0:8] = table
     table_ref[8:16] = rank
@@ -254,40 +256,64 @@
     for irrep in range(IRREPS):
         index_ref[irrep] = pick_rows(table, c_col ^ irrep)
     pack_rows(occ_s, t_ref, index_ref, rows_ref, t_all, tile)
-    pl.semaphore_wait(barrier, 5)
-    steps[0]()
-
-    sub = iota((wide, NV), 0)
-    lane = iota((wide, NV), 1)
-    of_d = spread(lane == sub // PART_A, col)
-    of_a = spread(lane == first_a + sub % PART_A, col)
-    both_irreps = of_d ^ of_a
-    for irrep in range(IRREPS):
-        v_index_ref[irrep] = pick_rows(table, both_irreps ^ irrep)
-    repeat = iota((NV, wide), 1) // PART_A == iota((NV, wide), 0)
+    pl.semaphore_wait(barrier, 8)
+    steps["begin"]()
+
     virt8 = jnp.broadcast_to(virt_ref[...], (8, NV))
+    repeat = iota((NV, 2 * NV), 1) // 2 == iota((NV, 2 * NV), 0)
     irrep_row = spread(virt8, repeat)[0:1]
     rank_row = spread(rank, repeat)[0:1]
-    at = iota((IRREPS * SLOTS, wide), 0)
-    perm_ref[...] = jnp.where((irrep_row == at // SLOTS) & (rank_row == at % SLOTS), 1.0, 0.0).astype(BF16)
-    steps[1]()
-
-    def prep(c, carry):
-        own = iota((wide, NV), 1) // SLOTS == iota((wide, NV), 0) % PART_A
-        irrep_c = virt_s[first_c + c]
-        got = lanes_at(v_all[c].astype(F32), v_index_ref[irrep_c])
-        compact = jnp.where(own, got, 0.0).astype(BF16)
-        ordered = jnp.dot(perm_ref[...], compact, preferred_element_type=F32).astype(BF16)
-        sorted_ref[...] = ordered.reshape(IRREPS, SLOTS, NV)
-        start = pl.multiple_of((c % 8) * NV + (c // 8) * SLOTS, SLOTS)
+    at = iota((2 * IRREPS * SLOTS, 2 * NV), 0)
+    par = iota((2 * IRREPS * SLOTS, 2 * NV), 1) % 2
+    wanted = (irrep_row == (at // SLOTS) % IRREPS) & (rank_row == at % SLOTS) & (par == at // (IRREPS * SLOTS))
+    perm_ref[...] = jnp.where(wanted, 1.0, 0.0).astype(BF16)
+
+    flat_v = v_all.reshape(2 * PART_C * 2 * NV, NV)
+
+    def sort_rows(c, carry):
+        right = jnp.concatenate(
+            [flat_v[pl.ds(pl.multiple_of((p * PART_C + c) * 2 * NV, 2 * NV), 2 * NV)] for p in range(2)], axis=1
+        )
+        ordered = jnp.dot(perm_ref[...], right, preferred_element_type=F32).astype(BF16)
+        x_all[c] = ordered.reshape(2, IRREPS, SLOTS, 2 * NV)
+        return carry
+
+    for copy in v_copies:
+        copy.wait()
+    lax.fori_loop(0, PART_C // 2, sort_rows, 0, unroll=4)
+    steps["near"]()
+    lax.fori_loop(PART_C // 2, PART_C, sort_rows, 0, unroll=4)
+    steps["far"]()
+
+    lane = iota((NV, NV), 1)
+    of_a = iota((NV, NV), 0) == first_a + lane // SLOTS
+    a_row = spread(virt8, of_a)[0:1]
+    mixed = jnp.where(rank_col == lane % SLOTS, col ^ a_row, -1)
+    for p in range(4):
+        a = 2 * (p % 2) + p // 2
+        mine = jnp.where(lane // SLOTS == a, mixed, -1)
         for irrep in range(IRREPS):
-            right_ref[irrep // 2, pl.ds(start, SLOTS), (irrep % 2) * NV : (irrep % 2 + 1) * NV] = sorted_ref[irrep_c ^ irrep]
+            slot_ref[irrep, p * NV : (p + 1) * NV] = jnp.where(mine == irrep, 1.0, 0.0).astype(BF16)
+
+    def pick_slots(pair, carry):
+        for odd in range(2):
+            irrep = 2 * pair + odd
+            for q in range(4):
+                blocks = []
+                for m in range(8):
+                    c = 8 * q + m
+                    which = virt_s[first_c + c] ^ irrep
+                    blocks.append(jnp.concatenate([x_all[c, 0, which], x_all[c, 1, which]], axis=1))
+                got = jnp.dot(jnp.concatenate(blocks, axis=0), slot_ref[irrep], preferred_element_type=F32).astype(BF16)
+                for m in range(8):
+                    start = m * NV + q * SLOTS
+                    right_ref[pair, start : start + SLOTS, odd * NV : (odd + 1) * NV] = got[m * SLOTS : (m + 1) * SLOTS]
         return carry
 
-    for n in range(PART_C // C_STEP):
-        v_copies[n].wait()
-        lax.fori_loop(C_STEP * n, C_STEP * (n + 1), prep, 0)
-        steps[2 + n]()
+    lax.fori_loop(0, 2, pick_slots, 0)
+    steps["second", 0]()
+    lax.fori_loop(2, 4, pick_slots, 0)
+    steps["second", -1]()
 
     occ_col = occupied_column(occ_s, 0, NO)
     subd = iota((NV, 2 * NV), 0)
@@ -302,39 +328,55 @@
     lane_at = iota(deep, 1)
     c_at = 8 * ((row_at % NV) // SLOTS) + row_at // NV
     wanted = (c_at == (lane_at // 2) % PART_C) & (lane_at % 2 == 0) & (a_rank == row_at % SLOTS)
-    cut = jnp.where(wanted, 1.0, 0.0).astype(BF16)
+    cut_one_ref[...] = jnp.where(wanted, 1.0, 0.0).astype(BF16)
     for a in range(PART_A):
         base = occ_col ^ a_irrep[0:1, 2 * a * PART_C : 2 * a * PART_C + 1]
         for irrep in range(IRREPS):
             c_index_ref[irrep, a * NO : (a + 1) * NO] = pick_rows(table, base ^ irrep)
-    for n in range(2 + PART_C // C_STEP, len(steps) - 1):
-        steps[n]()
-
-    chips = 4
-    m_rows = chips * 2 * ROWS
-
-    def ladder_block(n, carry):
-        got = t_all[pl.ds(n * 2 * chips, 2 * chips)].astype(F32)
+
+    each = 2 * ROWS
+
+    def ladder_pair(*origins):
+        for origin in origins:
+            steps["sibling"](origin)
+        chips = [ring.tile_of(dx, dz, 0) // 2 for dx, dz in origins]
+        slabs = [t_all[pl.ds(2 * chip, 2)].astype(F32) for chip in chips]
         planes = [
-            got[:, m // 2, :, (m % 2) * 8 : (m % 2) * 8 + 8].reshape(m_rows, NV).astype(BF16)
+            jnp.concatenate(
+                [got[:, m // 2, :, (m % 2) * 8 : (m % 2) * 8 + 8].reshape(each, NV) for got in slabs], axis=0
+            ).astype(BF16)
             for m in range(8)
         ]
         left = jnp.concatenate(planes, axis=1)
-        pair_irrep = jnp.concatenate([occ_col ^ occ_s[n * (m_rows // NO) + u] for u in range(m_rows // NO)], axis=0)
-        total = jnp.zeros((m_rows, NV), F32)
+        pair_irrep = jnp.concatenate([occ_col ^ occ_s[3 * chip + u] for chip in chips for u in range(3)], axis=0)
+        total = jnp.zeros((2 * each, NV), F32)
         for pair in range(4):
             both = jnp.dot(left, right_ref[pair], preferred_element_type=F32)
             total = jnp.where(pair_irrep == 2 * pair, both[:, :NV], total)
             total = jnp.where(pair_irrep == 2 * pair + 1, both[:, NV:], total)
-        rows = pl.ds(pl.multiple_of(n * m_rows, m_rows), m_rows)
-        ladder_ref[rows] = total
-        piece = jnp.dot(left, cut, preferred_element_type=F32)
-        for half in range(2):
-            lanes = slice(half * NV, (half + 1) * NV)
-            cut_ref[half, rows] = jnp.where(pair_irrep == ac_irrep[:, lanes], piece[:, lanes], 0.0)
-        return carry
-
-    lax.fori_loop(0, 16 // chips, ladder_block, 0)
+        piece = jnp.dot(left, cut_one_ref[...], preferred_element_type=F32)
+        for n, chip in enumerate(chips):
+            rows = pl.ds(pl.multiple_of(chip * each, each), each)
+            part = slice(n * each, (n + 1) * each)
+            ladder_ref[rows] = total[part]
+            for half in range(2):
+                lanes = slice(half * NV, (half + 1) * NV)
+                cut_ref[half, rows] = jnp.where(pair_irrep[part] == ac_irrep[:, lanes], piece[part, lanes], 0.0)
+
+    ladder_pair((0, 0), (1, 0))
+    steps["second", 1]()
+    ladder_pair((-1, 0), (0, 1))
+    steps["second", 2]()
+    ladder_pair((0, -1), (-1, -1))
+    steps["last", 0]()
+    ladder_pair((1, 1), (-1, 1))
+    steps["last", -1]()
+    steps["last", 1]()
+    ladder_pair((1, -1), (0, 2))
+    steps["last", 2]()
+    ladder_pair((2, 0), (1, 2))
+    ladder_pair((-1, 2), (2, 1))
+    ladder_pair((2, -1), (2, 2))
 
     lane48 = iota((NO, NV), 1)
     odd_half = lane48 // (2 * PART_C) == 1
@@ -352,18 +394,20 @@
                 left_ref[(PART_A + a) * NO : (PART_A + a + 1) * NO, lanes] = pltpu.roll(piece, 1, 1).astype(BF16)
         return carry
 
-    lax.fori_loop(0, JP, left_block, 0, unroll=2)
+    lax.fori_loop(0, JP, left_block, 0, unroll=4)
 
     flat = w_all.reshape(JP * 2 * KC, NV)
     span = 2 * NO
     for copy in w_copies:
         copy.wait()
 
-    def cycle_block(n, carry):
+    def cycle_product(n, out):
         right = jnp.concatenate(
             [flat[pl.ds(pl.multiple_of((n * JP_STEP + u) * 2 * KC, 2 * KC), 2 * KC)] for u in range(JP_STEP)], axis=1
         )
-        both = jnp.dot(left_ref[...], right, preferred_element_type=F32)
+        out[...] = jnp.dot(left_ref[...], right, preferred_element_type=F32)
+
+    def cycle_place(n, both):
         for u in range(JP_STEP):
             for odd in range(2):
                 j = (n * JP_STEP + u) * 2 + odd
@@ -376,78 +420,109 @@
                 start = pl.multiple_of(j * span, NO)
                 total_ref[pl.ds(start, NO)] = value
                 total_ref[pl.ds(start + NO, NO)] = value
+
+    cycle_product(0, both_a)
+
+    def cycle_pair(n, carry):
+        cycle_product(2 * n + 1, both_b)
+        cycle_place(2 * n, both_a)
+        cycle_product(2 * n + 2, both_a)
+        cycle_place(2 * n + 1, both_b)
         return carry
 
-    lax.fori_loop(0, JP // JP_STEP, cycle_block, 0)
+    blocks = JP // JP_STEP
+    lax.fori_loop(0, blocks // 2 - 1, cycle_pair, 0)
+    cycle_product(blocks - 1, both_b)
+    cycle_place(blocks - 2, both_a)
+    cycle_place(blocks - 1, both_b)
     total_ref[pl.ds(NO * span, TURN * span)] = total_ref[pl.ds(0, TURN * span)]
 
     def anti(j, carry):
         ahead = total_ref[pl.ds(j * span + j + 1, TURN, stride=1)]
         across = total_ref[pl.ds((j + 1) * span + j, TURN, stride=span)]
-        out_ref[j] = ahead - across
+        z_ref[j] = ahead - across
         return carry
 
     lax.fori_loop(0, NO, anti, 0, unroll=4)
-    steps[-1]()
-
-
-def contract(occ, virt, virt_row, amplitudes, ladder_rows, cycle_pairs):
-    wide = NV * PART_A
+    exchange_part(occ_s, virt8, table, rank, z_ref, own_ref, near_ref, far_ref, *exchange_refs)
+    steps["settle"]()
+
+
+def contract(occ, virt, virt_row, amplitudes, ladder_pairs, cycle_pairs):
     pairs = NO * NO
+    block = PART_J * PART_J
+    half = (PART_J // 2, TURN, NV)
     vmem = pl.BlockSpec(memory_space=pltpu.VMEM)
     smem = pl.BlockSpec(memory_space=pltpu.SMEM)
     hbm = pl.BlockSpec(memory_space=pl.ANY)
     return pl.pallas_call(
         contract_body,
         out_shape=(
-            jax.ShapeDtypeStruct((NO, TURN, NV), F32),
+            jax.ShapeDtypeStruct((OWN, NV), F32),
+            jax.ShapeDtypeStruct((block, NV), F32),
+            jax.ShapeDtypeStruct((FAR, NV), F32),
             jax.ShapeDtypeStruct((16, NV), I32),
         ),
         in_specs=[smem, smem, vmem, vmem, hbm, hbm],
-        out_specs=(vmem, vmem),
+        out_specs=(vmem, vmem, vmem, vmem),
         scratch_shapes=[
             pltpu.VMEM((TILES, 4, ROWS // 8, 16, NV), BF16),
             pltpu.VMEM((JP, KC, 2, NV), BF16),
-            pltpu.VMEM((PART_C, wide, NV), BF16),
-            pltpu.SemaphoreType.DMA((PART_C // C_STEP,)),
+            pltpu.VMEM((2, PART_C, NV, 2, NV), BF16),
+            pltpu.SemaphoreType.DMA((2,)),
             pltpu.SemaphoreType.DMA((JP,)),
             pltpu.SemaphoreType.DMA((TRANSFERS,)),
             pltpu.SemaphoreType.DMA((TRANSFERS,)),
             pltpu.VMEM((IRREPS, PART_C, NV), I32),
             pltpu.VMEM((NV, NV), I32),
             pltpu.VMEM((ROWS * 8, NV), F32),
-            pltpu.VMEM((IRREPS, wide, NV), I32),
-            pltpu.VMEM((IRREPS * SLOTS, wide), BF16),
-            pltpu.VMEM((IRREPS, SLOTS, NV), BF16),
+            pltpu.VMEM((2 * IRREPS * SLOTS, 2 * NV), BF16),
+            pltpu.VMEM((PART_C, 2, IRREPS, SLOTS, 2 * NV), BF16),
+            pltpu.VMEM((IRREPS, 4 * NV, NV), BF16),
             pltpu.VMEM((4, PART_C * SLOTS, 2 * NV), BF16),
+            pltpu.VMEM((PART_C * SLOTS, 2 * NV), BF16),
             pltpu.VMEM((pairs, NV), F32),
             pltpu.VMEM((2, pairs, NV), F32),
             pltpu.VMEM((2 * PART_A * NO, 2 * KC), BF16),
             pltpu.VMEM((IRREPS, PART_A * NO, NV), I32),
             pltpu.VMEM(((NO + TURN) * 2 * NO, NV), F32),
+            pltpu.VMEM((2 * PART_A * NO, JP_STEP * NV), F32),
+            pltpu.VMEM((2 * PART_A * NO, JP_STEP * NV), F32),
+            pltpu.VMEM((NO, TURN, NV), F32),
+            pltpu.VMEM((2,) + half, F32),
+            pltpu.VMEM((4,) + half, F32),
+            pltpu.VMEM((2,) + half, F32),
+            pltpu.VMEM((TILES, SHARE, NV), F32),
+            pltpu.VMEM((TILES * PITCH, NV), F32),
+            pltpu.VMEM((TILES, SHARE, NV), F32),
+            pltpu.VMEM((TILES * PITCH, NV), F32),
+            pltpu.VMEM((IRREPS, NV, NV), I32),
+            pltpu.VMEM((block, NV), F32),
+            pltpu.VMEM((FAR, NV), F32),
+            pltpu.SemaphoreType.DMA((6,)),
+            pltpu.SemaphoreType.DMA((6,)),
+            pltpu.SemaphoreType.DMA((TILES,)),
+            pltpu.SemaphoreType.DMA((TILES,)),
+            pltpu.SemaphoreType.DMA((TILES,)),
+            pltpu.SemaphoreType.DMA((TILES,)),
+            pltpu.SemaphoreType.DMA((2,)),
+            pltpu.SemaphoreType.DMA((2,)),
         ],
         compiler_params=pltpu.CompilerParams(
-            vmem_limit_bytes=60 * 2**20, collective_id=0, has_side_effects=True
+            vmem_limit_bytes=62 * 2**20, collective_id=0, has_side_effects=True
         ),
         name="contract",
-    )(occ, virt, virt_row, amplitudes, ladder_rows, cycle_pairs)
-
-
-def exchange_body(
-    occ_s, virt_ref, table_ref, z_ref, own_ref, near_ref, far_ref,
+    )(occ, virt, virt_row, amplitudes, ladder_pairs, cycle_pairs)
+
+
+def exchange_part(
+    occ_s, virt8, table, rank, z_ref, own_ref, near_ref, far_ref,
     stage_ref, direct_ref, merged_ref, first_ref, first_in, second_ref, second_in,
     index_ref, near_out, far_out, sum_send, sum_recv, a_send, a_recv, b_send, b_recv, f_send, f_recv,
 ):
     tile = lax.axis_index("tile")
     grp = lax.axis_index("grp")
     up, down, over = (grp + 1) % GRPS, (grp + 3) % GRPS, (grp + 2) % GRPS
-    barrier = pltpu.get_barrier_semaphore()
-    for target in (up, down, over):
-        pl.semaphore_signal(barrier, inc=1, device_id={"grp": target}, device_id_type=MESH)
-    for d in range(1, TILES):
-        pl.semaphore_signal(barrier, inc=1, device_id={"tile": (tile + d) % TILES}, device_id_type=MESH)
-    pl.semaphore_wait(barrier, TILES + 2)
-
     half = PART_J // 2
 
     def block(owner, part):
@@ -470,12 +545,11 @@
     for copy in sends[:4]:
         copy.start()
 
-    table = table_ref[0:8]
     sub = iota((NV, NV), 0)
     lane = iota((NV, NV), 1)
     turned = sub == 4 * (lane % SLOTS) + lane // SLOTS
-    rank_turned = spread(table_ref[8:16], turned)[0:1]
-    irrep_turned = spread(jnp.broadcast_to(virt_ref[...], (8, NV)), turned)[0:1]
+    rank_turned = spread(rank, turned)[0:1]
+    irrep_turned = spread(virt8, turned)[0:1]
     irrep_col = column_of(irrep_turned)
     table_turned = (table % 4) * SLOTS + table // 4
     for irrep in range(IRREPS):
@@ -532,7 +606,7 @@
             second_ref[t, pl.ds(n, 1)] = value[t : t + 1]
         return carry
 
-    lax.fori_loop(0, SHARE, one, 0)
+    lax.fori_loop(0, SHARE, one, 0, unroll=3)
     second_in[pl.ds(pl.multiple_of(tile * PITCH, PITCH), SHARE)] = second_ref[tile]
     more = swap_all(second_ref, second_in, b_send, b_recv)
     for copy in more:
@@ -541,7 +615,12 @@
         own_ref[u * SHARE : (u + 1) * SHARE] = second_in[u * PITCH : u * PITCH + SHARE]
     for x in range(PART_J):
         near_out[x * PART_J : (x + 1) * PART_J] = own_ref[x * TURN + 11 - x : x * TURN + 23 - x]
-        far_out[x * PART_J : (x + 1) * PART_J] = own_ref[x * TURN + 23 - x : x * TURN + 35 - x]
+    far_out[FAR - 8 : FAR] = jnp.zeros((8, NV), F32)
+    filled = 0
+    for y in range(PART_J - 1):
+        count = PART_J - 1 - y
+        far_out[filled : filled + count] = own_ref[pl.ds((y + 1) * (TURN - 1) + 23 + y, count, stride=TURN - 1)]
+        filled += count
     ends = [
         to("grp", up, near_out, near_ref, f_send.at[0], f_recv.at[0]),
         to("grp", over, far_out, far_ref, f_send.at[1], f_recv.at[1]),
@@ -552,47 +631,6 @@
         copy.wait_send()
     for copy in ends:
         copy.wait()
-
-
-def exchange(occ, virt_row, table, partial_sum):
-    vmem = pl.BlockSpec(memory_space=pltpu.VMEM)
-    smem = pl.BlockSpec(memory_space=pltpu.SMEM)
-    block = PART_J * PART_J
-    half = (PART_J // 2, TURN, NV)
-    return pl.pallas_call(
-        exchange_body,
-        out_shape=(
-            jax.ShapeDtypeStruct((OWN, NV), F32),
-            jax.ShapeDtypeStruct((block, NV), F32),
-            jax.ShapeDtypeStruct((block, NV), F32),
-        ),
-        in_specs=[smem, vmem, vmem, vmem],
-        out_specs=(vmem, vmem, vmem),
-        scratch_shapes=[
-            pltpu.VMEM((2,) + half, F32),
-            pltpu.VMEM((4,) + half, F32),
-            pltpu.VMEM((2,) + half, F32),
-            pltpu.VMEM((TILES, SHARE, NV), F32),
-            pltpu.VMEM((TILES * PITCH, NV), F32),
-            pltpu.VMEM((TILES, SHARE, NV), F32),
-            pltpu.VMEM((TILES * PITCH, NV), F32),
-            pltpu.VMEM((IRREPS, NV, NV), I32),
-            pltpu.VMEM((block, NV), F32),
-            pltpu.VMEM((block, NV), F32),
-            pltpu.SemaphoreType.DMA((6,)),
-            pltpu.SemaphoreType.DMA((6,)),
-            pltpu.SemaphoreType.DMA((TILES,)),
-            pltpu.SemaphoreType.DMA((TILES,)),
-            pltpu.SemaphoreType.DMA((TILES,)),
-            pltpu.SemaphoreType.DMA((TILES,)),
-            pltpu.SemaphoreType.DMA((2,)),
-            pltpu.SemaphoreType.DMA((2,)),
-        ],
-        compiler_params=pltpu.CompilerParams(
-            vmem_limit_bytes=32 * 2**20, collective_id=1, has_side_effects=True
-        ),
-        name="exchange",
-    )(occ, virt_row, table, partial_sum)
 
 
 def expand_body(occ_s, virt_ref, table_ref, own_ref, near_ref, far_ref, out_ref, rows_ref):
@@ -615,7 +653,8 @@
         at[n : 2 * n] = own_ref[x * TURN + 11 - x : x * TURN + 23 - x]
         at[2 * n : 2 * n + x + 1] = own_ref[x * TURN + 23 - x : x * TURN + 24]
         if x < n - 1:
-            at[2 * n + x + 1 : 3 * n] = -far_ref[pl.ds((x + 1) * n + x, n - 1 - x, stride=n)]
+            filled = x * (n - 1) - x * (x - 1) // 2
+            at[2 * n + x + 1 : 3 * n] = -far_ref[filled : filled + n - 1 - x]
         at[3 * n : 4 * n] = -near_ref[pl.ds(x, n, stride=n)]
     for x in range(n):
         rows = rows_ref[x]
@@ -644,11 +683,10 @@
 
 def shards(amplitudes, ladder_ints, cycle_ints, occ_irrep, virt_irrep):
     virt_row = virt_irrep.reshape(1, NV)
-    partial_sum, table = contract(
+    own, near, far, table = contract(
         occ_irrep, virt_irrep, virt_row, amplitudes,
-        ladder_ints.reshape(PART_C, NV * PART_A, NV), cycle_ints.reshape(KC, JP, 2, NV),
+        ladder_ints.reshape(PART_C, NV, 2, 2, NV), cycle_ints.reshape(KC, JP, 2, NV),
     )
-    own, near, far = exchange(occ_irrep, virt_row, table, partial_sum)
     return expand(occ_irrep, virt_row, table, own, near, far).reshape(NO, PART_J, PART_A, NV)
 
 

time: 94.3 us -> 82.7 us (0.88)
  Pallas kernels: 92.3 us -> 79.2 us
  local copies, waits for them, and re-layouts: 1.76 us -> 3.26 us
    pallas_call x2 -> x1, Pallas kernels: 89.9 us -> 76.8 us  [contract(): pl.pallas_call(contract_body, out_shape=(jax.ShapeDtypeStruct((OWN, NV),...]
    unnamed x8 -> x12, local copies, waits for them, and re-layouts: 1.76 us -> 3.26 us
where the time goes in v3:
time: 82.7 us; the launch traced here: 82.5 us
  Pallas kernels  79.2 us (96%)
  local copies, waits for them, and re-layouts  3.26 us (4%)
    pallas_call x1, Pallas kernels, contract(): pl.pallas_call(contract_body, out_shape=(jax.ShapeDtypeStruct((OWN, NV),...  76.8 us
    unnamed x12, local copies, waits for them, and re-layouts  3.26 us
    pallas_call x1, Pallas kernels, expand(): pl.pallas_call(expand_body, out_shape=jax.ShapeDtypeStruct((NO * PART_J *...  2.37 us

profile of v3, /device:TPU:1, one launch (start us, length us, event | category | flops | bytes accessed | tf_op | source)
XLA Modules:
  0.0 82.5 jit_solution(13809962443413196935)
XLA Ops:
  0.0 0.0 copy-start.4
  0.0 0.0 copy-start.5
  0.0 76.8 %contract.1 = (f32[288,128]{1,0:T(8,128)}, f32[144,128]{1,0:T(8,128)}, f32[72,128]{1,0:T(8,128)}, s32[16,128]{1,0:T(8,128)}) custom-call(s32[48]{0:T(128)} %occ_s.3, s32[128]{0:T(128)} %virt_s.1, s32[1,128]{1,0:T(1,128)} %bitcast.4, bf16[72,32,128]{2,1,0:T(8,128)(2,1)} %t_ref.1, bf16[32,128,2,2,128]{4,3,2,1,0:T(2,128)(2,1)} %bitcast.7, ...), custom_call_target="tpu_custom_call" | custom-call | tf_op jit(solution)/shard_map/contract/pallas_call | solution.py:458
  76.8 0.0 copy-done.4
  76.8 0.0 copy-done.5
  76.8 0.0 copy-start
  76.8 0.9 %copy-done = f32[288,128]{1,0:T(8,128)S(1)} copy-done((f32[288,128]{1,0:T(8,128)S(1)}, f32[288,128]{1,0:T(8,128)}, u32[]{:S(2)}) %copy-start) | copy-done | bytes 147480
  77.7 0.0 copy-start.1
  77.7 0.9 %copy-done.1 = f32[144,128]{1,0:T(8,128)S(1)} copy-done((f32[144,128]{1,0:T(8,128)S(1)}, f32[144,128]{1,0:T(8,128)}, u32[]{:S(2)}) %copy-start.1) | copy-done | bytes 73752
  78.6 0.0 copy-start.2
  78.6 0.8 copy-done.2
  79.4 0.0 copy-start.3
  79.4 0.7 copy-done.3
  80.1 2.4 %expand.1 = f32[2304,128]{1,0:T(8,128)} custom-call(s32[48]{0:T(128)S(1)} %copy-done.5, s32[1,128]{1,0:T(1,128)S(1)} %bitcast.5, s32[16,128]{1,0:T(8,128)S(1)} %copy-done.3, f32[288,128]{1,0:T(8,128)S(1)} %copy-done, f32[144,128]{1,0:T(8,128)S(1)} %copy-done.1, f32[72,128]{1,0:T(8,128)S(1)} %copy-done.2), custom_call_target="tpu_custom_call" | custom-call | tf_op jit(solution)/shard_map/expand/pallas_call | solution.py:673
Async XLA Ops:
  0.0 76.8 %copy-start.4 = (s32[128]{0:T(128)S(1)}, s32[128]{0:T(128)}, u32[]{:S(2)}) copy-start(s32[128]{0:T(128)} %virt_s.1) | copy-start | bytes 1540
  0.0 76.8 %copy-start.5 = (s32[48]{0:T(128)S(1)}, s32[48]{0:T(128)}, u32[]{:S(2)}) copy-start(s32[48]{0:T(128)} %occ_s.3) | copy-start | bytes 580
  76.8 0.9 %copy-start = (f32[288,128]{1,0:T(8,128)S(1)}, f32[288,128]{1,0:T(8,128)}, u32[]{:S(2)}) copy-start(f32[288,128]{1,0:T(8,128)} %get-tuple-element.10.own_ref) | copy-start | bytes 442372
  77.7 0.9 %copy-start.1 = (f32[144,128]{1,0:T(8,128)S(1)}, f32[144,128]{1,0:T(8,128)}, u32[]{:S(2)}) copy-start(f32[144,128]{1,0:T(8,128)} %get-tuple-element.11.near_ref) | copy-start | bytes 221188
  78.6 0.8 copy-start.2
  79.4 0.7 copy-start.3

commit v4 on v3

--- a/solution.py
+++ b/solution.py
@@ -1,3 +1,5 @@
+import functools
+
 import jax
 import jax.numpy as jnp
 from jax import lax
@@ -99,42 +101,56 @@
             out_ref[me, half, block] = jnp.concatenate(pair_of, axis=0).astype(BF16)
 
 
+PAIRED = (
+    ((0, 0), (1, 0)), ((-1, 0), (0, 1)), ((0, -1), (-1, -1)), ((1, 1), (-1, 1)),
+    ((1, -1), (0, 2)), ((2, 0), (1, 2)), ((-1, 2), (2, 1)), ((2, -1), (2, 2)),
+)
+RING_COPIES = 40
+
+
 class Ring:
     def __init__(self, t_all, send_sem, recv_sem):
         tile = lax.axis_index("tile")
         self.at = (tile // 8, (tile // 2) % 4, tile % 2)
         self.buffer, self.send_sem, self.recv_sem = t_all, send_sem, recv_sem
         self.named = {}
-        self.started = []
+        self.pair_of = {origin: n for n, pair in enumerate(PAIRED) for origin in pair}
 
     def tile_of(self, dx, dz, core):
         x, z, _ = self.at
         return ((x + dx + 4) % 4 * 4 + (z + dz + 4) % 4) * 2 + core
 
-    def copy(self, name, origin, parts, target, core_of):
-        number = self.named.setdefault(name, len(self.named))
-        block = self.buffer.at[self.tile_of(origin[0], origin[1], core_of), parts[0] : parts[1]]
+    def copy(self, number, origin, parts, target):
+        block = self.buffer.at[self.tile_of(origin[0], origin[1], self.at[2]), parts[0] : parts[1]]
         return pltpu.make_async_remote_copy(
             src_ref=block,
             dst_ref=block,
-            send_sem=self.send_sem.at[number],
+            send_sem=self.send_sem,
             recv_sem=self.recv_sem.at[number],
             device_id={"tile": target},
             device_id_type=MESH,
         )
 
+    def number(self, name):
+        return self.named.setdefault(name, len(self.named))
+
     def send(self, name, origin, parts, step):
-        core = self.at[2]
-        if step is None:
-            copy = self.copy(name, origin, parts, self.tile_of(0, 0, 1 - core), core)
-        else:
-            copy = self.copy(name, origin, parts, self.tile_of(step[0], step[1], core), core)
-        copy.start()
-        self.started.append(copy)
-
-    def arrive(self, name, origin, parts, core_of=None):
-        core = self.at[2]
-        self.copy(name, origin, parts, self.tile_of(0, 0, 1 - core), core if core_of is None else core_of).wait_recv()
+        self.copy(self.number(name), origin, parts, self.tile_of(step[0], step[1], self.at[2])).start()
+
+    def share(self, origin, parts):
+        number = RING_COPIES + self.pair_of[origin]
+        self.copy(number, origin, parts, self.tile_of(0, 0, 1 - self.at[2])).start()
+
+    def arrive(self, name, origin, parts):
+        self.copy(self.number(name), origin, parts, self.tile_of(0, 0, 1 - self.at[2])).wait_recv()
+
+    def shared(self, pair):
+        whole = self.buffer.at[0:2]
+        pltpu.make_async_copy(whole, whole, self.recv_sem.at[RING_COPIES + pair]).wait()
+
+    def settle(self):
+        whole = self.buffer.at[0 : TILES - 1]
+        pltpu.make_async_copy(whole, whole, self.send_sem).wait()
 
 
 def gather_steps(ring):
@@ -155,12 +171,12 @@
             for step in (1, -1):
                 ring.send((family, "s", 0, step), (0, 0), both(family), place(family, 0, step))
         for family in range(2):
-            ring.send((family, "c", 0, 0), (0, 0), both(family), None)
+            ring.share((0, 0), both(family))
 
     def spread_first(family, k):
         for step in (1, -1):
             ring.send((family, "s", k, step), place(family, k, 0), both(family), place(family, 0, step))
-        ring.send((family, "c", k, 0), place(family, k, 0), both(family), None)
+        ring.share(place(family, k, 0), both(family))
 
     def near():
         for family in range(2):
@@ -185,7 +201,7 @@
                     origin = place(family, k, -step)
                     ring.arrive((family, "s", k, step), origin, both(family))
                     ring.send((family, "t", k, step), origin, part(family, 0 if step == 1 else 1), place(family, 0, step))
-                    ring.send((family, "c", k, -step), origin, both(family), None)
+                    ring.share(origin, both(family))
 
         return run
 
@@ -194,36 +210,28 @@
             for family in range(2):
                 for step in (1, -1):
                     ring.arrive((family, "t", k, step), place(family, k, 2), part(family, 0 if step == 1 else 1))
-                ring.send((family, "c", k, 2), place(family, k, 2), both(family), None)
+                ring.share(place(family, k, 2), both(family))
 
         return run
 
-    def sibling(origin):
-        for family in range(2):
-            k, m = place(family, origin[0], origin[1])
-            ring.arrive((family, "c", k, m), origin, both(family), 1 - ring.at[2])
-
-    def settle():
-        for copy in ring.started:
-            copy.wait_send()
-
-    steps = {"begin": begin, "near": near, "far": far, "sibling": sibling, "settle": settle}
+    steps = {"begin": begin, "near": near, "far": far}
     for k in (0, -1, 1, 2):
         steps["second", k] = second(k)
         steps["last", k] = last(k)
     return steps
 
 
-TRANSFERS = 72
 KC = NO * PART_C
 JP = NO // 2
 JP_STEP = 4
 FAR = 72
+BLOCK = PART_J * PART_J
+OUT_ROWS = OWN + BLOCK + FAR + 16
 
 
 def contract_body(
-    occ_s, virt_s, virt_ref, t_ref, v_hbm, w_hbm, own_ref, near_ref, far_ref, table_ref,
-    t_all, w_all, v_all, v_sem, w_sem, send_sem, recv_sem,
+    occ_s, virt_s, virt_ref, t_hbm, v_hbm, w_hbm, out_ref,
+    t_ref, t_all, w_all, v_all, t_sem, v_sem, w_sem, send_sem, recv_sem,
     index_ref, column_ref, rows_ref, perm_ref, x_all, slot_ref, right_ref, cut_one_ref,
     ladder_ref, cut_ref, left_ref, c_index_ref, total_ref, both_a, both_b, z_ref, *exchange_refs,
 ):
@@ -231,10 +239,13 @@
     grp = lax.axis_index("grp")
     first_a = tile * PART_A
     first_c = grp * PART_C
-    v_copies = [pltpu.make_async_copy(v_hbm.at[:, :, n], v_all.at[n], v_sem.at[n]) for n in range(2)]
-    w_copies = [pltpu.make_async_copy(w_hbm.at[:, n], w_all.at[n], w_sem.at[n]) for n in range(JP)]
-    for copy in v_copies + w_copies:
-        copy.start()
+    own_ref = out_ref.at[0:OWN]
+    near_ref = out_ref.at[OWN : OWN + BLOCK]
+    far_ref = out_ref.at[OWN + BLOCK : OWN + BLOCK + FAR]
+    t_copy = pltpu.make_async_copy(t_hbm, t_ref, t_sem)
+    t_copy.start()
+    for n in range(2):
+        pltpu.make_async_copy(v_hbm.at[:, :, n], v_all.at[n], v_sem).start()
 
     ring = Ring(t_all, send_sem, recv_sem)
     steps = gather_steps(ring)
@@ -250,11 +261,12 @@
 
     col, table, rank, rank_col = slot_tables(virt_ref[...])
     column_ref[...] = col
-    table_ref[0:8] = table
-    table_ref[8:16] = rank
+    out_ref[OUT_ROWS - 16 : OUT_ROWS - 8] = table.astype(F32)
+    out_ref[OUT_ROWS - 8 : OUT_ROWS] = rank.astype(F32)
     c_col = column_ref[pl.ds(pl.multiple_of(first_c, PART_C), PART_C)]
     for irrep in range(IRREPS):
         index_ref[irrep] = pick_rows(table, c_col ^ irrep)
+    t_copy.wait()
     pack_rows(occ_s, t_ref, index_ref, rows_ref, t_all, tile)
     pl.semaphore_wait(barrier, 8)
     steps["begin"]()
@@ -278,13 +290,14 @@
         x_all[c] = ordered.reshape(2, IRREPS, SLOTS, 2 * NV)
         return carry
 
-    for copy in v_copies:
-        copy.wait()
-    lax.fori_loop(0, PART_C // 2, sort_rows, 0, unroll=4)
+    pltpu.make_async_copy(v_all, v_all, v_sem).wait()
+    for n in range(JP):
+        pltpu.make_async_copy(w_hbm.at[:, n], w_all.at[n], w_sem).start()
+    lax.fori_loop(0, PART_C // 4, sort_rows, 0, unroll=8)
     steps["near"]()
-    lax.fori_loop(PART_C // 2, PART_C, sort_rows, 0, unroll=4)
+    lax.fori_loop(PART_C // 4, PART_C // 2, sort_rows, 0, unroll=8)
     steps["far"]()
-
+    lax.fori_loop(PART_C // 2, PART_C, sort_rows, 0, unroll=8)
     lane = iota((NV, NV), 1)
     of_a = iota((NV, NV), 0) == first_a + lane // SLOTS
     a_row = spread(virt8, of_a)[0:1]
@@ -336,9 +349,9 @@
 
     each = 2 * ROWS
 
-    def ladder_pair(*origins):
-        for origin in origins:
-            steps["sibling"](origin)
+    def ladder_pair(number):
+        origins = PAIRED[number]
+        ring.shared(number)
         chips = [ring.tile_of(dx, dz, 0) // 2 for dx, dz in origins]
         slabs = [t_all[pl.ds(2 * chip, 2)].astype(F32) for chip in chips]
         planes = [
@@ -363,20 +376,19 @@
                 lanes = slice(half * NV, (half + 1) * NV)
                 cut_ref[half, rows] = jnp.where(pair_irrep[part] == ac_irrep[:, lanes], piece[part, lanes], 0.0)
 
-    ladder_pair((0, 0), (1, 0))
+    ladder_pair(0)
     steps["second", 1]()
-    ladder_pair((-1, 0), (0, 1))
+    ladder_pair(1)
     steps["second", 2]()
-    ladder_pair((0, -1), (-1, -1))
+    ladder_pair(2)
     steps["last", 0]()
-    ladder_pair((1, 1), (-1, 1))
+    ladder_pair(3)
     steps["last", -1]()
     steps["last", 1]()
-    ladder_pair((1, -1), (0, 2))
+    ladder_pair(4)
     steps["last", 2]()
-    ladder_pair((2, 0), (1, 2))
-    ladder_pair((-1, 2), (2, 1))
-    ladder_pair((2, -1), (2, 2))
+    for number in range(5, 8):
+        ladder_pair(number)
 
     lane48 = iota((NO, NV), 1)
     odd_half = lane48 // (2 * PART_C) == 1
@@ -398,8 +410,7 @@
 
     flat = w_all.reshape(JP * 2 * KC, NV)
     span = 2 * NO
-    for copy in w_copies:
-        copy.wait()
+    pltpu.make_async_copy(w_all, w_all, w_sem).wait()
 
     def cycle_product(n, out):
         right = jnp.concatenate(
@@ -445,34 +456,30 @@
 
     lax.fori_loop(0, NO, anti, 0, unroll=4)
     exchange_part(occ_s, virt8, table, rank, z_ref, own_ref, near_ref, far_ref, *exchange_refs)
-    steps["settle"]()
+    ring.settle()
 
 
 def contract(occ, virt, virt_row, amplitudes, ladder_pairs, cycle_pairs):
     pairs = NO * NO
-    block = PART_J * PART_J
     half = (PART_J // 2, TURN, NV)
     vmem = pl.BlockSpec(memory_space=pltpu.VMEM)
     smem = pl.BlockSpec(memory_space=pltpu.SMEM)
     hbm = pl.BlockSpec(memory_space=pl.ANY)
     return pl.pallas_call(
         contract_body,
-        out_shape=(
-            jax.ShapeDtypeStruct((OWN, NV), F32),
-            jax.ShapeDtypeStruct((block, NV), F32),
-            jax.ShapeDtypeStruct((FAR, NV), F32),
-            jax.ShapeDtypeStruct((16, NV), I32),
-        ),
-        in_specs=[smem, smem, vmem, vmem, hbm, hbm],
-        out_specs=(vmem, vmem, vmem, vmem),
+        out_shape=jax.ShapeDtypeStruct((OUT_ROWS, NV), F32),
+        in_specs=[smem, smem, vmem, hbm, hbm, hbm],
+        out_specs=vmem,
         scratch_shapes=[
+            pltpu.VMEM((ROWS, PART_C, NV), BF16),
             pltpu.VMEM((TILES, 4, ROWS // 8, 16, NV), BF16),
             pltpu.VMEM((JP, KC, 2, NV), BF16),
             pltpu.VMEM((2, PART_C, NV, 2, NV), BF16),
-            pltpu.SemaphoreType.DMA((2,)),
-            pltpu.SemaphoreType.DMA((JP,)),
-            pltpu.SemaphoreType.DMA((TRANSFERS,)),
-            pltpu.SemaphoreType.DMA((TRANSFERS,)),
+            pltpu.SemaphoreType.DMA,
+            pltpu.SemaphoreType.DMA,
+            pltpu.SemaphoreType.DMA,
+            pltpu.SemaphoreType.DMA,
+            pltpu.SemaphoreType.DMA((RING_COPIES + len(PAIRED),)),
             pltpu.VMEM((IRREPS, PART_C, NV), I32),
             pltpu.VMEM((NV, NV), I32),
             pltpu.VMEM((ROWS * 8, NV), F32),
@@ -497,14 +504,14 @@
             pltpu.VMEM((TILES, SHARE, NV), F32),
             pltpu.VMEM((TILES * PITCH, NV), F32),
             pltpu.VMEM((IRREPS, NV, NV), I32),
-            pltpu.VMEM((block, NV), F32),
+            pltpu.VMEM((BLOCK, NV), F32),
             pltpu.VMEM((FAR, NV), F32),
             pltpu.SemaphoreType.DMA((6,)),
             pltpu.SemaphoreType.DMA((6,)),
-            pltpu.SemaphoreType.DMA((TILES,)),
-            pltpu.SemaphoreType.DMA((TILES,)),
-            pltpu.SemaphoreType.DMA((TILES,)),
-            pltpu.SemaphoreType.DMA((TILES,)),
+            pltpu.SemaphoreType.DMA,
+            pltpu.SemaphoreType.DMA,
+            pltpu.SemaphoreType.DMA,
+            pltpu.SemaphoreType.DMA,
             pltpu.SemaphoreType.DMA((2,)),
             pltpu.SemaphoreType.DMA((2,)),
         ],
@@ -542,8 +549,8 @@
         to("grp", up, merged_ref.at[0], direct_ref.at[2], sum_send.at[4], sum_recv.at[4]),
         to("grp", down, merged_ref.at[1], direct_ref.at[3], sum_send.at[5], sum_recv.at[5]),
     ]
-    for copy in sends[:4]:
-        copy.start()
+    for number in (0, 3, 1):
+        sends[number].start()
 
     sub = iota((NV, NV), 0)
     lane = iota((NV, NV), 1)
@@ -555,36 +562,42 @@
     for irrep in range(IRREPS):
         index_ref[irrep] = pick_rows(table_turned, irrep_col ^ irrep)
 
+    def swap(src, dst, send, recv, target):
+        to("tile", target, src.at[target], dst.at[pl.ds(pl.multiple_of(tile * PITCH, PITCH), SHARE)], send, recv).start()
+
+    def swapped(dst, sem):
+        rows = dst.at[0 : (TILES - 1) * SHARE]
+        pltpu.make_async_copy(rows, rows, sem).wait()
+
+    def first_half(part, value):
+        own_ref[part * OWN // 2 : (part + 1) * OWN // 2] = value.reshape(OWN // 2, NV)
+        near_tiles = TILES // 2
+        for u in range(part * near_tiles, (part + 1) * near_tiles):
+            first_ref[u] = own_ref[u * SHARE : (u + 1) * SHARE]
+        for d in range(near_tiles):
+            target = part * near_tiles + (tile + d) % near_tiles
+            if d == 0:
+                pl.when(tile // near_tiles != part)(
+                    functools.partial(swap, first_ref, first_in, a_send, a_recv, target)
+                )
+            else:
+                swap(first_ref, first_in, a_send, a_recv, target)
+
     sends[0].wait_recv()
     merged_ref[0] = stage_ref[0] + z_ref[block(up, 0)]
     sends[4].start()
+    sends[2].start()
     sends[1].wait_recv()
     merged_ref[1] = stage_ref[1] + z_ref[block(down, 1)]
     sends[5].start()
-    sends[2].wait_recv()
     sends[3].wait_recv()
     sends[4].wait_recv()
+    first_half(0, z_ref[block(grp, 0)] + direct_ref[1] + direct_ref[2])
+    sends[2].wait_recv()
     sends[5].wait_recv()
-    lower = z_ref[block(grp, 0)] + direct_ref[1] + direct_ref[2]
-    upper = z_ref[block(grp, 1)] + direct_ref[0] + direct_ref[3]
-    own_ref[0 : OWN // 2] = lower.reshape(OWN // 2, NV)
-    own_ref[OWN // 2 : OWN] = upper.reshape(OWN // 2, NV)
-    for u in range(TILES):
-        first_ref[u] = own_ref[u * SHARE : (u + 1) * SHARE]
-
-    def swap_all(src, dst, send, recv):
-        copies = []
-        for d in range(1, TILES):
-            target = (tile + d) % TILES
-            copy = to("tile", target, src.at[target], dst.at[pl.ds(pl.multiple_of(tile * PITCH, PITCH), SHARE)], send.at[d], recv.at[d])
-            copy.start()
-            copies.append(copy)
-        return copies
-
+    first_half(1, z_ref[block(grp, 1)] + direct_ref[0] + direct_ref[3])
     first_in[pl.ds(pl.multiple_of(tile * PITCH, PITCH), SHARE)] = first_ref[tile]
-    copies = swap_all(first_ref, first_in, a_send, a_recv)
-    for copy in copies:
-        copy.wait_recv()
+    swapped(first_in, a_recv)
 
     quarter = iota((TILES, NV), 1) // SLOTS
 
@@ -608,9 +621,9 @@
 
     lax.fori_loop(0, SHARE, one, 0, unroll=3)
     second_in[pl.ds(pl.multiple_of(tile * PITCH, PITCH), SHARE)] = second_ref[tile]
-    more = swap_all(second_ref, second_in, b_send, b_recv)
-    for copy in more:
-        copy.wait_recv()
+    for d in range(1, TILES):
+        swap(second_ref, second_in, b_send, b_recv, (tile + d) % TILES)
+    swapped(second_in, b_recv)
     for u in range(TILES):
         own_ref[u * SHARE : (u + 1) * SHARE] = second_in[u * PITCH : u * PITCH + SHARE]
     for x in range(PART_J):
@@ -627,19 +640,24 @@
     ]
     for copy in ends:
         copy.start()
-    for copy in sends + copies + more:
+    for copy in sends:
         copy.wait_send()
+    swapped(first_in, a_send)
+    swapped(second_in, b_send)
     for copy in ends:
         copy.wait()
 
 
-def expand_body(occ_s, virt_ref, table_ref, own_ref, near_ref, far_ref, out_ref, rows_ref):
+def expand_body(occ_s, virt_ref, in_ref, out_ref, rows_ref):
+    own_ref = in_ref.at[0:OWN]
+    near_ref = in_ref.at[OWN : OWN + BLOCK]
+    far_ref = in_ref.at[OWN + BLOCK : OWN + BLOCK + FAR]
     first_a = lax.axis_index("tile") * PART_A
     grp = lax.axis_index("grp")
     first_j = grp * PART_J
     occ_col = occupied_column(occ_s, first_j, NO)
     virt_row = jnp.broadcast_to(virt_ref[...], (NO, NV))
-    rank_row = jnp.broadcast_to(table_ref[8:9], (NO, NV))
+    rank_row = jnp.broadcast_to(in_ref[OUT_ROWS - 8 : OUT_ROWS - 7], (NO, NV)).astype(I32)
     virt8 = jnp.broadcast_to(virt_ref[...], (8, NV))
     a_irrep = spread(virt8, iota((NV, NV), 0) == first_a + iota((NV, NV), 1) // PART_C)
     n = PART_J
@@ -668,26 +686,26 @@
                 out_ref[pl.ds(start, n, stride=n * PART_A)] = value[b * n : (b + 1) * n]
 
 
-def expand(occ, virt_row, table, own, near, far):
+def expand(occ, virt_row, compact):
     vmem = pl.BlockSpec(memory_space=pltpu.VMEM)
     return pl.pallas_call(
         expand_body,
         out_shape=jax.ShapeDtypeStruct((NO * PART_J * PART_A, NV), F32),
-        in_specs=[pl.BlockSpec(memory_space=pltpu.SMEM)] + [vmem] * 5,
+        in_specs=[pl.BlockSpec(memory_space=pltpu.SMEM), vmem, vmem],
         out_specs=vmem,
         scratch_shapes=[pltpu.VMEM((PART_J, NO, NV), F32)],
         compiler_params=pltpu.CompilerParams(vmem_limit_bytes=32 * 2**20),
         name="expand",
-    )(occ, virt_row, table, own, near, far)
+    )(occ, virt_row, compact)
 
 
 def shards(amplitudes, ladder_ints, cycle_ints, occ_irrep, virt_irrep):
     virt_row = virt_irrep.reshape(1, NV)
-    own, near, far, table = contract(
+    compact = contract(
         occ_irrep, virt_irrep, virt_row, amplitudes,
         ladder_ints.reshape(PART_C, NV, 2, 2, NV), cycle_ints.reshape(KC, JP, 2, NV),
     )
-    return expand(occ_irrep, virt_row, table, own, near, far).reshape(NO, PART_J, PART_A, NV)
+    return expand(occ_irrep, virt_row, compact).reshape(NO, PART_J, PART_A, NV)
 
 
 def solution(mesh):

time: 82.7 us -> 75.2 us (0.909)
  Pallas kernels: 79.2 us -> 74.1 us
  local copies, waits for them, and re-layouts: 3.26 us -> 0.95 us
    pallas_call x1, Pallas kernels: 76.8 us -> 71.7 us  [contract(): pl.pallas_call(contract_body, out_shape=jax.ShapeDtypeStruct((OUT_ROWS, N...]
    unnamed x12 -> x6, local copies, waits for them, and re-layouts: 3.26 us -> 0.95 us
where the time goes in v4:
time: 75.2 us; the launch traced here: 75.1 us
  Pallas kernels  74.1 us (99%)
  local copies, waits for them, and re-layouts  0.95 us (1%)
    pallas_call x1, Pallas kernels, contract(): pl.pallas_call(contract_body, out_shape=jax.ShapeDtypeStruct((OUT_ROWS, N...  71.7 us
    pallas_call x1, Pallas kernels, expand(): pl.pallas_call(expand_body, out_shape=jax.ShapeDtypeStruct((NO * PART_J *...  2.37 us

profile of v4, /device:TPU:1, one launch (start us, length us, event | category | flops | bytes accessed | tf_op | source)
XLA Modules:
  0.0 75.1 jit_solution(5620839568196227757)
XLA Ops:
  0.0 0.0 copy-start.1
  0.0 0.0 copy-start.2
  0.0 71.7 %contract.1.in_ref = f32[520,128]{1,0:T(8,128)} custom-call(s32[48]{0:T(128)} %occ_s.3, s32[128]{0:T(128)} %virt_s.1, s32[1,128]{1,0:T(1,128)} %bitcast.4, bf16[72,32,128]{2,1,0:T(8,128)(2,1)} %t_hbm.1, bf16[32,128,2,2,128]{4,3,2,1,0:T(2,128)(2,1)} %bitcast.7, bf16[1536,24,2,128]{3,2,1,0:T(2,128)(2,1)} %bitcast.6), custom_call_target="tpu_custom_call" | custom-call | tf_op jit(solution)/shard_map/contract/pallas_call | solution.py:468
  71.7 0.0 copy-done.1
  71.8 0.0 copy-done.2
  71.8 0.0 copy-start
  71.8 0.9 %copy-done = f32[520,128]{1,0:T(8,128)S(1)} copy-done((f32[520,128]{1,0:T(8,128)S(1)}, f32[520,128]{1,0:T(8,128)}, u32[]{:S(2)}) %copy-start) | copy-done | bytes 266264
  72.7 2.4 %expand.1 = f32[2304,128]{1,0:T(8,128)} custom-call(s32[48]{0:T(128)S(1)} %copy-done.2, s32[1,128]{1,0:T(1,128)S(1)} %bitcast.5, f32[520,128]{1,0:T(8,128)S(1)} %copy-done), custom_call_target="tpu_custom_call" | custom-call | tf_op jit(solution)/shard_map/expand/pallas_call | solution.py:691
Async XLA Ops:
  0.0 71.7 %copy-start.1 = (s32[128]{0:T(128)S(1)}, s32[128]{0:T(128)}, u32[]{:S(2)}) copy-start(s32[128]{0:T(128)} %virt_s.1) | copy-start | bytes 1540
  0.0 71.8 %copy-start.2 = (s32[48]{0:T(128)S(1)}, s32[48]{0:T(128)}, u32[]{:S(2)}) copy-start(s32[48]{0:T(128)} %occ_s.3) | copy-start | bytes 580
  71.8 1.0 %copy-start = (f32[520,128]{1,0:T(8,128)S(1)}, f32[520,128]{1,0:T(8,128)}, u32[]{:S(2)}) copy-start(f32[520,128]{1,0:T(8,128)} %contract.1.in_ref) | copy-start | bytes 798724

commit v5 on v4

--- a/solution.py
+++ b/solution.py
@@ -105,7 +105,7 @@
     ((0, 0), (1, 0)), ((-1, 0), (0, 1)), ((0, -1), (-1, -1)), ((1, 1), (-1, 1)),
     ((1, -1), (0, 2)), ((2, 0), (1, 2)), ((-1, 2), (2, 1)), ((2, -1), (2, 2)),
 )
-RING_COPIES = 40
+RING_COPIES = 38
 
 
 class Ring:
@@ -167,6 +167,7 @@
         for family in range(2):
             ring.send((family, "f", 1), (0, 0), both(family), place(family, 1, 0))
             ring.send((family, "f", -1), (0, 0), both(family), place(family, -1, 0))
+            ring.send((family, "g"), (0, 0), both(family), place(family, 2, 0))
         for family in range(2):
             for step in (1, -1):
                 ring.send((family, "s", 0, step), (0, 0), both(family), place(family, 0, step))
@@ -183,15 +184,13 @@
             for step in (1, -1):
                 origin = place(family, -step, 0)
                 ring.arrive((family, "f", step), origin, both(family))
-                ring.send((family, "g", step), origin, part(family, 0 if step == 1 else 1), place(family, step, 0))
         for family in range(2):
             for k in (-1, 1):
                 spread_first(family, k)
 
     def far():
         for family in range(2):
-            for step in (1, -1):
-                ring.arrive((family, "g", step), place(family, 2, 0), part(family, 0 if step == 1 else 1))
+            ring.arrive((family, "g"), place(family, 2, 0), both(family))
             spread_first(family, 2)
 
     def second(k):
@@ -224,9 +223,9 @@
 KC = NO * PART_C
 JP = NO // 2
 JP_STEP = 4
-FAR = 72
-BLOCK = PART_J * PART_J
-OUT_ROWS = OWN + BLOCK + FAR + 16
+OUT_ROWS = 3 * OWN + 16
+NEAR_TILES = sorted({(TURN * x + 11 + y - x) // SHARE for x in range(PART_J) for y in range(PART_J)})
+FAR_TILES = sorted({(TURN * x + 23 + y - x) // SHARE for x in range(PART_J) for y in range(x)})
 
 
 def contract_body(
@@ -240,8 +239,8 @@
     first_a = tile * PART_A
     first_c = grp * PART_C
     own_ref = out_ref.at[0:OWN]
-    near_ref = out_ref.at[OWN : OWN + BLOCK]
-    far_ref = out_ref.at[OWN + BLOCK : OWN + BLOCK + FAR]
+    near_ref = out_ref.at[OWN : 2 * OWN]
+    far_ref = out_ref.at[2 * OWN : 3 * OWN]
     t_copy = pltpu.make_async_copy(t_hbm, t_ref, t_sem)
     t_copy.start()
     for n in range(2):
@@ -253,7 +252,7 @@
     barrier = pltpu.get_barrier_semaphore()
     for target in (
         ring.tile_of(1, 0, core), ring.tile_of(-1, 0, core), ring.tile_of(0, 1, core),
-        ring.tile_of(0, -1, core), ring.tile_of(0, 0, 1 - core),
+        ring.tile_of(0, -1, core), ring.tile_of(0, 0, 1 - core), ring.tile_of(2, 0, core), ring.tile_of(0, 2, core),
     ):
         pl.semaphore_signal(barrier, inc=1, device_id={"tile": target}, device_id_type=MESH)
     for d in range(1, GRPS):
@@ -268,7 +267,7 @@
         index_ref[irrep] = pick_rows(table, c_col ^ irrep)
     t_copy.wait()
     pack_rows(occ_s, t_ref, index_ref, rows_ref, t_all, tile)
-    pl.semaphore_wait(barrier, 8)
+    pl.semaphore_wait(barrier, 10)
     steps["begin"]()
 
     virt8 = jnp.broadcast_to(virt_ref[...], (8, NV))
@@ -376,19 +375,20 @@
                 lanes = slice(half * NV, (half + 1) * NV)
                 cut_ref[half, rows] = jnp.where(pair_irrep[part] == ac_irrep[:, lanes], piece[part, lanes], 0.0)
 
+    steps["second", 1]()
     ladder_pair(0)
-    steps["second", 1]()
+    steps["second", 2]()
     ladder_pair(1)
-    steps["second", 2]()
     ladder_pair(2)
     steps["last", 0]()
     ladder_pair(3)
+    ladder_pair(4)
     steps["last", -1]()
     steps["last", 1]()
-    ladder_pair(4)
+    ladder_pair(5)
     steps["last", 2]()
-    for number in range(5, 8):
-        ladder_pair(number)
+    ladder_pair(6)
+    ladder_pair(7)
 
     lane48 = iota((NO, NV), 1)
     odd_half = lane48 // (2 * PART_C) == 1
@@ -496,18 +496,16 @@
             pltpu.VMEM((2 * PART_A * NO, JP_STEP * NV), F32),
             pltpu.VMEM((2 * PART_A * NO, JP_STEP * NV), F32),
             pltpu.VMEM((NO, TURN, NV), F32),
-            pltpu.VMEM((2,) + half, F32),
-            pltpu.VMEM((4,) + half, F32),
-            pltpu.VMEM((2,) + half, F32),
+            pltpu.VMEM((2, 3) + half, F32),
             pltpu.VMEM((TILES, SHARE, NV), F32),
             pltpu.VMEM((TILES * PITCH, NV), F32),
             pltpu.VMEM((TILES, SHARE, NV), F32),
             pltpu.VMEM((TILES * PITCH, NV), F32),
             pltpu.VMEM((IRREPS, NV, NV), I32),
-            pltpu.VMEM((BLOCK, NV), F32),
-            pltpu.VMEM((FAR, NV), F32),
-            pltpu.SemaphoreType.DMA((6,)),
-            pltpu.SemaphoreType.DMA((6,)),
+            pltpu.VMEM((TILES * PITCH, NV), F32),
+            pltpu.VMEM((TILES * PITCH, NV), F32),
+            pltpu.SemaphoreType.DMA((2, 3)),
+            pltpu.SemaphoreType.DMA((2, 3)),
             pltpu.SemaphoreType.DMA,
             pltpu.SemaphoreType.DMA,
             pltpu.SemaphoreType.DMA,
@@ -524,8 +522,8 @@
 
 def exchange_part(
     occ_s, virt8, table, rank, z_ref, own_ref, near_ref, far_ref,
-    stage_ref, direct_ref, merged_ref, first_ref, first_in, second_ref, second_in,
-    index_ref, near_out, far_out, sum_send, sum_recv, a_send, a_recv, b_send, b_recv, f_send, f_recv,
+    direct_ref, first_ref, first_in, second_ref, second_in,
+    index_ref, near_in, far_in, sum_send, sum_recv, a_send, a_recv, b_send, b_recv, f_send, f_recv,
 ):
     tile = lax.axis_index("tile")
     grp = lax.axis_index("grp")
@@ -542,15 +540,12 @@
         )
 
     sends = [
-        to("grp", up, z_ref.at[block(over, 0)], stage_ref.at[0], sum_send.at[0], sum_recv.at[0]),
-        to("grp", down, z_ref.at[block(over, 1)], stage_ref.at[1], sum_send.at[1], sum_recv.at[1]),
-        to("grp", up, z_ref.at[block(up, 1)], direct_ref.at[0], sum_send.at[2], sum_recv.at[2]),
-        to("grp", down, z_ref.at[block(down, 0)], direct_ref.at[1], sum_send.at[3], sum_recv.at[3]),
-        to("grp", up, merged_ref.at[0], direct_ref.at[2], sum_send.at[4], sum_recv.at[4]),
-        to("grp", down, merged_ref.at[1], direct_ref.at[3], sum_send.at[5], sum_recv.at[5]),
+        to("grp", peer, z_ref.at[block(peer, part)], direct_ref.at[part, n], sum_send.at[part, n], sum_recv.at[part, n])
+        for part in range(2)
+        for n, peer in enumerate((over, up, down))
     ]
-    for number in (0, 3, 1):
-        sends[number].start()
+    for copy in sends:
+        copy.start()
 
     sub = iota((NV, NV), 0)
     lane = iota((NV, NV), 1)
@@ -583,19 +578,10 @@
             else:
                 swap(first_ref, first_in, a_send, a_recv, target)
 
-    sends[0].wait_recv()
-    merged_ref[0] = stage_ref[0] + z_ref[block(up, 0)]
-    sends[4].start()
-    sends[2].start()
-    sends[1].wait_recv()
-    merged_ref[1] = stage_ref[1] + z_ref[block(down, 1)]
-    sends[5].start()
-    sends[3].wait_recv()
-    sends[4].wait_recv()
-    first_half(0, z_ref[block(grp, 0)] + direct_ref[1] + direct_ref[2])
-    sends[2].wait_recv()
-    sends[5].wait_recv()
-    first_half(1, z_ref[block(grp, 1)] + direct_ref[0] + direct_ref[3])
+    for part in range(2):
+        for copy in sends[3 * part : 3 * part + 3]:
+            copy.wait_recv()
+        first_half(part, z_ref[block(grp, part)] + direct_ref[part, 0] + direct_ref[part, 1] + direct_ref[part, 2])
     first_in[pl.ds(pl.multiple_of(tile * PITCH, PITCH), SHARE)] = first_ref[tile]
     swapped(first_in, a_recv)
 
@@ -620,38 +606,48 @@
         return carry
 
     lax.fori_loop(0, SHARE, one, 0, unroll=3)
-    second_in[pl.ds(pl.multiple_of(tile * PITCH, PITCH), SHARE)] = second_ref[tile]
+    def forward(dst, number, peer):
+        for d in range(TILES):
+            target = (tile + d) % TILES
+            pltpu.make_async_remote_copy(
+                src_ref=second_ref.at[target],
+                dst_ref=dst.at[pl.ds(pl.multiple_of(tile * PITCH, PITCH), SHARE)],
+                send_sem=f_send.at[number], recv_sem=f_recv.at[number],
+                device_id={"tile": target, "grp": peer}, device_id_type=MESH,
+            ).start()
+
+    def taken(dst, sem, tiles):
+        rows = dst.at[0 : tiles * SHARE]
+        pltpu.make_async_copy(rows, rows, sem).wait()
+
+    in_near = functools.reduce(lambda one, two: one | two, [tile == u for u in NEAR_TILES])
+    in_far = functools.reduce(lambda one, two: one | two, [tile == u for u in FAR_TILES])
+    pl.when(in_far)(lambda: forward(far_in, 1, over))
+    pl.when(in_near)(lambda: forward(near_in, 0, up))
     for d in range(1, TILES):
         swap(second_ref, second_in, b_send, b_recv, (tile + d) % TILES)
+    second_in[pl.ds(pl.multiple_of(tile * PITCH, PITCH), SHARE)] = second_ref[tile]
     swapped(second_in, b_recv)
     for u in range(TILES):
         own_ref[u * SHARE : (u + 1) * SHARE] = second_in[u * PITCH : u * PITCH + SHARE]
-    for x in range(PART_J):
-        near_out[x * PART_J : (x + 1) * PART_J] = own_ref[x * TURN + 11 - x : x * TURN + 23 - x]
-    far_out[FAR - 8 : FAR] = jnp.zeros((8, NV), F32)
-    filled = 0
-    for y in range(PART_J - 1):
-        count = PART_J - 1 - y
-        far_out[filled : filled + count] = own_ref[pl.ds((y + 1) * (TURN - 1) + 23 + y, count, stride=TURN - 1)]
-        filled += count
-    ends = [
-        to("grp", up, near_out, near_ref, f_send.at[0], f_recv.at[0]),
-        to("grp", over, far_out, far_ref, f_send.at[1], f_recv.at[1]),
-    ]
-    for copy in ends:
-        copy.start()
+    taken(near_in, f_recv.at[0], len(NEAR_TILES))
+    for u in NEAR_TILES:
+        near_ref[u * SHARE : (u + 1) * SHARE] = near_in[u * PITCH : u * PITCH + SHARE]
+    taken(far_in, f_recv.at[1], len(FAR_TILES))
+    for u in FAR_TILES:
+        far_ref[u * SHARE : (u + 1) * SHARE] = far_in[u * PITCH : u * PITCH + SHARE]
     for copy in sends:
         copy.wait_send()
     swapped(first_in, a_send)
     swapped(second_in, b_send)
-    for copy in ends:
-        copy.wait()
+    pl.when(in_near)(lambda: taken(near_in, f_send.at[0], TILES))
+    pl.when(in_far)(lambda: taken(far_in, f_send.at[1], TILES))
 
 
 def expand_body(occ_s, virt_ref, in_ref, out_ref, rows_ref):
     own_ref = in_ref.at[0:OWN]
-    near_ref = in_ref.at[OWN : OWN + BLOCK]
-    far_ref = in_ref.at[OWN + BLOCK : OWN + BLOCK + FAR]
+    near_ref = in_ref.at[OWN : 2 * OWN]
+    far_ref = in_ref.at[2 * OWN : 3 * OWN]
     first_a = lax.axis_index("tile") * PART_A
     grp = lax.axis_index("grp")
     first_j = grp * PART_J
@@ -671,9 +667,9 @@
         at[n : 2 * n] = own_ref[x * TURN + 11 - x : x * TURN + 23 - x]
         at[2 * n : 2 * n + x + 1] = own_ref[x * TURN + 23 - x : x * TURN + 24]
         if x < n - 1:
-            filled = x * (n - 1) - x * (x - 1) // 2
-            at[2 * n + x + 1 : 3 * n] = -far_ref[filled : filled + n - 1 - x]
-        at[3 * n : 4 * n] = -near_ref[pl.ds(x, n, stride=n)]
+            start = (TURN - 1) * (x + 1) + 23 + x
+            at[2 * n + x + 1 : 3 * n] = -far_ref[pl.ds(start, n - 1 - x, stride=TURN - 1)]
+        at[3 * n : 4 * n] = -near_ref[pl.ds(11 + x, n, stride=TURN - 1)]
     for x in range(n):
         rows = rows_ref[x]
         irrep_j = occ_s[first_j + x]

time: 75.2 us -> 75.1 us (level)
  no operation moved by 1% of the time
where the time goes in v5:
time: 75.1 us; the launch traced here: 75 us
  Pallas kernels  73.9 us (98%)
  local copies, waits for them, and re-layouts  1.02 us (1%)
    pallas_call x1, Pallas kernels, contract(): pl.pallas_call(contract_body, out_shape=jax.ShapeDtypeStruct((OUT_ROWS, N...  71.6 us
    pallas_call x1, Pallas kernels, expand(): pl.pallas_call(expand_body, out_shape=jax.ShapeDtypeStruct((NO * PART_J *...  2.37 us

profile of v5, /device:TPU:1, one launch (start us, length us, event | category | flops | bytes accessed | tf_op | source)
XLA Modules:
  0.0 75.0 jit_solution(8013464874834401448)
XLA Ops:
  0.0 0.0 copy-start.1
  0.0 0.0 copy-start.2
  0.0 71.6 %contract.1.in_ref = f32[880,128]{1,0:T(8,128)} custom-call(s32[48]{0:T(128)} %occ_s.3, s32[128]{0:T(128)} %virt_s.1, s32[1,128]{1,0:T(1,128)} %bitcast.4, bf16[72,32,128]{2,1,0:T(8,128)(2,1)} %t_hbm.1, bf16[32,128,2,2,128]{4,3,2,1,0:T(2,128)(2,1)} %bitcast.7, bf16[1536,24,2,128]{3,2,1,0:T(2,128)(2,1)} %bitcast.6), custom_call_target="tpu_custom_call" | custom-call | tf_op jit(solution)/shard_map/contract/pallas_call | solution.py:468
  71.6 0.0 copy-done.1
  71.6 0.0 copy-done.2
  71.6 0.0 copy-start
  71.6 1.0 %copy-done = f32[880,128]{1,0:T(8,128)S(1)} copy-done((f32[880,128]{1,0:T(8,128)S(1)}, f32[880,128]{1,0:T(8,128)}, u32[]{:S(2)}) %copy-start) | copy-done | bytes 450584
  72.6 2.4 %expand.1 = f32[2304,128]{1,0:T(8,128)} custom-call(s32[48]{0:T(128)S(1)} %copy-done.2, s32[1,128]{1,0:T(1,128)S(1)} %bitcast.5, f32[880,128]{1,0:T(8,128)S(1)} %copy-done), custom_call_target="tpu_custom_call" | custom-call | tf_op jit(solution)/shard_map/expand/pallas_call | solution.py:687
Async XLA Ops:
  0.0 71.6 %copy-start.1 = (s32[128]{0:T(128)S(1)}, s32[128]{0:T(128)}, u32[]{:S(2)}) copy-start(s32[128]{0:T(128)} %virt_s.1) | copy-start | bytes 1540
  0.0 71.6 %copy-start.2 = (s32[48]{0:T(128)S(1)}, s32[48]{0:T(128)}, u32[]{:S(2)}) copy-start(s32[48]{0:T(128)} %occ_s.3) | copy-start | bytes 580
  71.6 1.0 %copy-start = (f32[880,128]{1,0:T(8,128)S(1)}, f32[880,128]{1,0:T(8,128)}, u32[]{:S(2)}) copy-start(f32[880,128]{1,0:T(8,128)} %contract.1.in_ref) | copy-start | bytes 1351684

commit v6 on v5

--- a/solution.py
+++ b/solution.py
@@ -644,7 +644,9 @@
     pl.when(in_far)(lambda: taken(far_in, f_send.at[1], TILES))
 
 
-def expand_body(occ_s, virt_ref, in_ref, out_ref, rows_ref):
+def expand_body(occ_s, virt_ref, in_hbm, out_ref, rows_ref, in_ref, in_sem):
+    in_copy = pltpu.make_async_copy(in_hbm, in_ref, in_sem)
+    in_copy.start()
     own_ref = in_ref.at[0:OWN]
     near_ref = in_ref.at[OWN : 2 * OWN]
     far_ref = in_ref.at[2 * OWN : 3 * OWN]
@@ -653,9 +655,10 @@
     first_j = grp * PART_J
     occ_col = occupied_column(occ_s, first_j, NO)
     virt_row = jnp.broadcast_to(virt_ref[...], (NO, NV))
-    rank_row = jnp.broadcast_to(in_ref[OUT_ROWS - 8 : OUT_ROWS - 7], (NO, NV)).astype(I32)
     virt8 = jnp.broadcast_to(virt_ref[...], (8, NV))
     a_irrep = spread(virt8, iota((NV, NV), 0) == first_a + iota((NV, NV), 1) // PART_C)
+    in_copy.wait()
+    rank_row = jnp.broadcast_to(in_ref[OUT_ROWS - 8 : OUT_ROWS - 7], (NO, NV)).astype(I32)
     n = PART_J
     for x in range(n):
         at = rows_ref.at[x]
@@ -687,10 +690,14 @@
     return pl.pallas_call(
         expand_body,
         out_shape=jax.ShapeDtypeStruct((NO * PART_J * PART_A, NV), F32),
-        in_specs=[pl.BlockSpec(memory_space=pltpu.SMEM), vmem, vmem],
+        in_specs=[pl.BlockSpec(memory_space=pltpu.SMEM), vmem, pl.BlockSpec(memory_space=pl.ANY)],
         out_specs=vmem,
-        scratch_shapes=[pltpu.VMEM((PART_J, NO, NV), F32)],
-        compiler_params=pltpu.CompilerParams(vmem_limit_bytes=32 * 2**20),
+        scratch_shapes=[
+            pltpu.VMEM((PART_J, NO, NV), F32),
+            pltpu.VMEM((OUT_ROWS, NV), F32),
+            pltpu.SemaphoreType.DMA,
+        ],
+        compiler_params=pltpu.CompilerParams(vmem_limit_bytes=62 * 2**20),
         name="expand",
     )(occ, virt_row, compact)
 

time: 75.1 us -> 75.3 us (level)
  Pallas kernels: 73.9 us -> 75 us
  local copies, waits for them, and re-layouts: 1.02 us -> 0 us
    pallas_call x1, Pallas kernels: 2.37 us -> 3.51 us  [expand(): pl.pallas_call(expand_body, out_shape=jax.ShapeDtypeStruct((NO * PART_J *...]
    unnamed x6 -> x0, local copies, waits for them, and re-layouts: 1.02 us -> none
where the time goes in v6:
time: 75.3 us; the launch traced here: 75.1 us
  Pallas kernels  75 us (100%)
    pallas_call x1, Pallas kernels, contract(): pl.pallas_call(contract_body, out_shape=jax.ShapeDtypeStruct((OUT_ROWS, N...  71.4 us
    pallas_call x1, Pallas kernels, expand(): pl.pallas_call(expand_body, out_shape=jax.ShapeDtypeStruct((NO * PART_J *...  3.51 us

profile of v6, /device:TPU:1, one launch (start us, length us, event | category | flops | bytes accessed | tf_op | source)
XLA Modules:
  0.0 75.1 jit_solution(7240207027397544268)
XLA Ops:
  0.0 71.4 %contract.1.in_hbm = f32[880,128]{1,0:T(8,128)} custom-call(s32[48]{0:T(128)} %occ_s.3, s32[128]{0:T(128)} %virt_s.1, s32[1,128]{1,0:T(1,128)} %bitcast.6, bf16[72,32,128]{2,1,0:T(8,128)(2,1)} %t_hbm.1, bf16[32,128,2,2,128]{4,3,2,1,0:T(2,128)(2,1)} %bitcast.5, bf16[1536,24,2,128]{3,2,1,0:T(2,128)(2,1)} %bitcast.4), custom_call_target="tpu_custom_call" | custom-call | tf_op jit(solution)/shard_map/contract/pallas_call | solution.py:468
  71.5 3.5 %expand.1 = f32[2304,128]{1,0:T(8,128)} custom-call(s32[48]{0:T(128)} %occ_s.3, s32[1,128]{1,0:T(1,128)} %bitcast.7, f32[880,128]{1,0:T(8,128)} %contract.1.in_hbm), custom_call_target="tpu_custom_call" | custom-call | tf_op jit(solution)/shard_map/expand/pallas_call | solution.py:690
